TPU v7x, 32 devices: a whole 2x2x4 slice. The times are simulated.
32 devices in a mesh: row: 8 (over z, core), col: 4 (over y, x).
Axes of the slice: x: 2, y: 2, z: 4, core: 2. Of those that a mesh axis runs over, the one named last changes fastest.
Arguments:
- blocks: bfloat16 [256, 16, 128, 128], P('row', 'col'), may hold values from -0.8984375 to 0.8984375
- pattern: int32 [256, 16], replicated, may hold values from 0 to 255, as said below
- anchors: int32 [3, 256, 16], replicated, may hold values from 0 to 127, as said below
- basis_x: bfloat16 [16, 128], replicated, may hold values from -0.5 to 0.5
- basis_yz: bfloat16 [128, 256], replicated, may hold values from -0.5 to 0.5
Outputs:
- square: float32 [256, 16, 128, 128], P('row', 'col')
- grid_values: float32 [128, 128, 128], P('row', 'col')
Inputs may be any that keep to these rules, and one draw needn't show every extreme that they name: pattern[i,k] = (i + d) mod 256 with -8 <= d <= 8; the 16 columns of a row are distinct. For block row i in group g = i // 32, anchors[0,i,k] = (g * 16 - 16 / 2 + u) mod 128 with 0 <= u <= 16; anchors[1,i,k] <= 112; anchors[2,i,k] <= 112.
All inputs are finite; a program needn't handle non-finite values.
Results may differ from a plain program's by a relative error of at most 0.0041.
Values may be sent and summed in bfloat16 or wider, within the bound.
No kernel may reach another device: no remote copies, remote signals or barrier semaphores. Data moves between devices by JAX's collectives and lax.ppermute only.
A program may use at most 128 MiB of HBM per device.

v0:
```python
import math

import jax
import jax.numpy as jnp
from jax import lax
from jax.sharding import PartitionSpec as P

H = 8
PL = 16
GY = 128
GZ = 128
TX = 16
TY = 16
TZ = 16


def from_behind(value, axis, by):
    peers = lax.axis_size(axis)
    return lax.ppermute(value, axis, [(i, (i + by) % peers) for i in range(peers)])


def extended_2(cells, sides, width):
    for axis, dim in sides:
        count = lax.axis_size(axis)
        head = lax.slice_in_dim(cells, 0, width, axis=dim)
        tail = lax.slice_in_dim(cells, cells.shape[dim] - width, cells.shape[dim], axis=dim)
        cells = jnp.concatenate(
            [
                lax.ppermute(tail, axis, [(i, (i + 1) % count) for i in range(count)]),
                cells,
                lax.ppermute(head, axis, [((i + 1) % count, i) for i in range(count)]),
            ],
            axis=dim,
        )
    return cells


def fold_rims(slab, margin):
    upper_rim = slab[slab.shape[0] - margin :]
    lower_rim = slab[:margin]
    from_below = from_behind(upper_rim, "row", 1)
    from_above = from_behind(lower_rim, "row", -1)
    interior = slab[margin : slab.shape[0] - margin]
    interior = interior.at[:margin].add(from_below)
    interior = interior.at[interior.shape[0] - margin :].add(from_above)
    return interior


def share_sums(slab):
    return lax.psum_scatter(slab, "col", scatter_dimension=1, tiled=True)


def per_device(blocks, pattern, anchors, basis_x, basis_yz):
    rows_dev, slots, bsize, _ = blocks.shape
    kslots = pattern.shape[1]
    row_count = lax.axis_size("row")
    row_place = lax.axis_index("row")
    col_place = lax.axis_index("col")
    total_rows = rows_dev * row_count
    full_rows = lax.all_gather(blocks, "col", axis=1, tiled=True)
    extended = extended_2(full_rows, (("row", 0),), H)
    span_rows = rows_dev + 2 * H
    stacked = jnp.concatenate(
        [
            extended.reshape(span_rows * kslots, bsize, bsize),
            jnp.zeros((1, bsize, bsize), jnp.bfloat16),
        ],
        axis=0,
    )
    first_row = row_place * rows_dev
    own_pattern = lax.dynamic_slice_in_dim(pattern, first_row, rows_dev, 0)
    own_targets = lax.dynamic_slice_in_dim(own_pattern, col_place * slots, slots, 1)
    slot_ids = jnp.arange(kslots, dtype=jnp.int32)

    def one_row(row_local):
        columns = own_pattern[row_local]
        targets = own_targets[row_local]
        far_pattern = pattern[columns]
        matches = (far_pattern[:, :, None] == targets[None, None, :]).astype(jnp.int32)
        matched = jnp.sum(matches, axis=1)
        match_slot = jnp.sum(matches * slot_ids[None, :, None], axis=1)
        local_row = (columns - first_row + H) % total_rows
        block_index = jnp.where(
            matched > 0, local_row[:, None] * kslots + match_slot, span_rows * kslots
        )
        picked = stacked[block_index]
        left_blocks = lax.dynamic_index_in_dim(extended, row_local + H, 0, keepdims=False)
        return jnp.einsum("kmn,ksnp->smp", left_blocks, picked, preferred_element_type=jnp.float32)

    square = lax.map(one_row, jnp.arange(rows_dev, dtype=jnp.int32))
    density = square.astype(jnp.bfloat16)
    task_count = rows_dev * slots
    density_rows = density.reshape(task_count, bsize, bsize)
    halves = jnp.einsum(
        "am,qmn->qan", basis_x, density_rows, preferred_element_type=jnp.float32
    ).astype(jnp.bfloat16)
    tile_values = jnp.einsum(
        "qan,nc->qac", halves, basis_yz, preferred_element_type=jnp.float32
    ).reshape(task_count, TX, TY, TZ)
    own_anchors = lax.dynamic_slice(
        anchors, (0, first_row, col_place * slots), (3, rows_dev, slots)
    ).reshape(3, task_count)
    margin = TX // 2
    grid_planes = PL * row_count
    slab_planes = PL + 2 * margin
    first_cells = (own_anchors[0] - row_place * PL + margin) % grid_planes
    grid_y = GY
    grid_z = GZ
    batch_size = math.gcd(task_count, 8)
    batch_count = task_count // batch_size
    tile_batches = tile_values.reshape(batch_count, batch_size, TX, TY, TZ)
    plane_starts = first_cells.reshape(batch_count, batch_size)
    row_starts = own_anchors[1].reshape(batch_count, batch_size)
    cell_starts = own_anchors[2].reshape(batch_count, batch_size)
    highest = lax.Precision.HIGHEST

    def place_batch(slab, inputs):
        tiles, plane_first, row_first, cell_first = inputs
        plane_cells = plane_first[:, None] + jnp.arange(TX, dtype=jnp.int32)[None, :]
        plane_pick = (
            plane_cells[:, :, None] == jnp.arange(slab_planes, dtype=jnp.int32)[None, None, :]
        ).astype(jnp.float32)
        row_cells = row_first[:, None] + jnp.arange(TY, dtype=jnp.int32)[None, :]
        row_pick = (
            row_cells[:, :, None] == jnp.arange(grid_y, dtype=jnp.int32)[None, None, :]
        ).astype(jnp.float32)
        depth_cells = cell_first[:, None] + jnp.arange(TZ, dtype=jnp.int32)[None, :]
        cell_pick = (
            depth_cells[:, :, None] == jnp.arange(grid_z, dtype=jnp.int32)[None, None, :]
        ).astype(jnp.float32)
        placed_z = jnp.einsum("qabc,qcz->qabz", tiles, cell_pick, precision=highest)
        placed_y = jnp.einsum("qby,qabz->qayz", row_pick, placed_z, precision=highest)
        return (slab + jnp.einsum("qap,qayz->pyz", plane_pick, placed_y, precision=highest), None)

    partial_grid, _ = lax.scan(
        place_batch,
        jnp.zeros((slab_planes, grid_y, grid_z), jnp.float32),
        (tile_batches, plane_starts, row_starts, cell_starts),
    )
    grid_values = share_sums(fold_rims(partial_grid, margin))
    return (square, grid_values)


def solution(mesh):
    placed = (P("row", "col", None, None), P(), P(), P(), P())
    return jax.shard_map(
        per_device,
        mesh=mesh,
        in_specs=placed,
        out_specs=(P("row", "col", None, None), P("row", "col", None)),
        check_vma=False,
    )
```

profile of v0, /device:TPU:0, one launch (start us, length us, event | category | flops | bytes accessed | tf_op | source)
XLA Modules:
  0.0 1313.7 jit_solution(1490450810987815775)
XLA Ops:
  8.0 162.0 %all-gather.2.cloned.1.call-done = bf16[32,16,128,128]{3,2,1,0:T(8,128)(2,1)} async-done(((bf16[32,4,128,128]{3,2,1,0:T(8,128)(2,1)}), bf16[32,16,128,128]{3,2,1,0:T(8,128)(2,1)}) %all-gather.2.cloned.1.call-update) | async-done | bytes 16777232 | tf_op jit(solution)/shard_map/all_gather | solution.py:60
  181.2 88.1 %collective-permute-done = bf16[8,16,128,128]{3,2,1,0:T(8,128)(2,1)} collective-permute-done((bf16[8,16,128,128]{3,2,1,0:T(8,128)(2,1)}, bf16[8,16,128,128]{3,2,1,0:T(8,128)(2,1)}, u32[]{:S(2)}, u32[]{:S(2)}) %collective-permute-start) | collective-permute-done | bytes 4194336 | tf_op jit(solution)/shard_map/ppermute | solution.py:29
  283.9 16.9 %concatenate.11 = bf16[769,128,128]{2,1,0:T(8,128)(2,1)} pad(bf16[768,128,128]{2,1,0:T(8,128)(2,1)S(1)} %bitcast.120, bf16[]{:T(256)} %constant.189.clone.1), padding=0_1x0_0x0_0 | pad | bytes 50364416 | tf_op jit(solution)/shard_map/concatenate | solution.py:63
  300.7 530.3 %while.26 = (s32[]{:T(128)}, f32[32,4,128,128]{2,3,1,0:T(8,128)}, s32[32]{0:T(128)S(1)}, s32[32,16]{1,0:T(8,128)S(1)}, s32[256,16]{1,0:T(8,128)S(1)}, /*index=5*...) while((s32[]{:T(128)}, f32[32,4,128,128]{2,3,1,0:T(8,128)}, ...), condition=%wide.region_3.4_spmd.clone, body=%wide.region_0.3_spmd.clone.sunk | while | flops 268443168 | bytes 7093221 | solution.py:90
  838.4 10.6 reshape_reshape.3
  849.0 415.0 %while.27 = (s32[]{:T(128)}, f32[32,128,128]{2,0,1:T(8,128)S(1)}, s32[16,8]{1,0:T(8,128)S(1)}, f32[16,8,16,16,16]{4,3,1,0,2:T(8,128)}, s32[16,8]{1,0:T(8,128)S(1...) while((s32[]{:T(128)}, f32[32,128,128]{2,0,1:T(8,128)S(1)}, s32[16,8]{1,0:T(8,128)S(1)}, ...), condition=%wide.region_5.6_spmd.clone, body=%wide.region_4.5_spmd.clone.sunk | while | flops 1259377024 | bytes 40898436 | solution.py:135
  860.0 9.2 copy.68
  886.0 9.2 copy.68
  911.9 9.2 copy.68
  937.8 9.2 copy.68
  963.8 9.2 copy.68
  989.7 9.2 copy.68
  1015.6 9.2 copy.68
  1041.6 9.2 copy.68
  1067.5 9.2 copy.68
  1093.4 9.2 copy.68
  1119.4 9.2 copy.68
  1145.3 9.2 copy.68
  1171.3 9.2 copy.68
  1197.2 9.2 copy.68
  1223.1 9.2 copy.68
  1249.1 9.2 copy.68
  1269.0 11.6 collective-permute-done.2
  1290.8 16.1 %reduce-scatter.2.cloned.1.call-done = f32[16,32,128]{2,1,0:T(8,128)} async-done(((f32[16,128,128]{2,1,0:T(8,128)}), f32[16,32,128]{2,1,0:T(8,128)}) %reduce-scatter.2.cloned.1.call-update) | async-done | bytes 262160 | tf_op jit(solution)/shard_map/reduce_scatter | solution.py:50
  (595 shorter events, 741.3 us)
Async XLA Ops:
  7.2 829.4 %copy-start = (bf16[128,256]{1,0:T(8,128)(2,1)S(1)}, bf16[128,256]{1,0:T(8,128)(2,1)}, u32[]{:S(2)}) copy-start(bf16[128,256]{1,0:T(8,128)(2,1)} %param.17) | copy-start | bytes 196612
  7.2 162.8 %all-gather.2.cloned.1.call-start = ((), (), s32[]{:S(2)}) async-start(), calls=%async_computation.1 | async-start | bytes 20971520 | tf_op jit(solution)/shard_map/all_gather | solution.py:60
  7.9 171.8 %copy-start.5 = (s32[256,16]{0,1:T(8,128)S(1)}, s32[256,16]{0,1:T(8,128)}, u32[]{:S(2)}) copy-start(s32[256,16]{0,1:T(8,128)} %param.14) | copy-start | bytes 49156
  7.9 1299.0 %reduce-scatter.2.cloned.1.call-start = ((), (), s32[]{:S(2)}) async-start(), calls=%async_computation.2 | async-start | bytes 1310720 | tf_op jit(solution)/shard_map/reduce_scatter | solution.py:50
  176.2 93.1 %collective-permute-start = (bf16[8,16,128,128]{3,2,1,0:T(8,128)(2,1)}, bf16[8,16,128,128]{3,2,1,0:T(8,128)(2,1)}, u32[]{:S(2)}, u32[]{:S(2)}) collective-permute-start(bf16[8,16,128,128]{3,2,1,0:T(8,128)(2,1)} %get-tuple-element.314), channel_id=1, source_target_pairs={{0,4},{4,8},{8,12},{12,16},{16,20},{20,24},{24,28},{28,0},{1,5},{5... | collective-permute-start | bytes 12582920 | tf_op jit(solution)/shard_map/ppermute | solution.py:29
  176.2 104.6 %collective-permute-start.1 = (bf16[8,16,128,128]{3,2,1,0:T(8,128)(2,1)}, bf16[8,16,128,128]{3,2,1,0:T(8,128)(2,1)}, u32[]{:S(2)}, u32[]{:S(2)}) collective-permute-start(bf16[8,16,128,128]{3,2,1,0:T(8,128)(2,1)} %get-tuple-element.313), channel_id=1, source_target_pairs={{4,0},{8,4},{12,8},{16,12},{20,16},{24,20},{28,24},{0,28},{5,1},{9... | collective-permute-start | bytes 12582920 | tf_op jit(solution)/shard_map/ppermute | solution.py:31
  283.9 16.9 %copy-start.3 = (bf16[48,16,128,128]{3,2,1,0:T(8,128)(2,1)}, bf16[48,16,128,128]{3,2,1,0:T(8,128)(2,1)S(1)}, u32[]{:S(2)}) copy-start(bf16[48,16,128,128]{3,2,1,0:T(8,128)(2,1)S(1)} %constant_dynamic-update-slice_fusion) | copy-start | bytes 75497472
  831.0 4.4 copy-start.6
  838.4 10.6 copy-start.2
  1265.3 15.3 %collective-permute-start.2 = (f32[8,128,128]{2,1,0:T(8,128)S(1)}, f32[8,128,128]{2,1,0:T(8,128)S(1)}, u32[]{:S(2)}, u32[]{:S(2)}) collective-permute-start(f32[8,128,128]{2,1,0:T(8,128)S(1)} %get-tuple-element.316), channel_id=1, source_target_pairs={{0,4},{4,8},{8,12},{12,16},{16,20},{20,24},{24,28},{28,0},{1,5},{5... | collective-permute-start | bytes 1572872 | tf_op jit(solution)/shard_map/ppermute | solution.py:19
  1265.3 15.3 %collective-permute-start.3 = (f32[8,128,128]{2,1,0:T(8,128)S(1)}, f32[8,128,128]{2,1,0:T(8,128)S(1)}, u32[]{:S(2)}, u32[]{:S(2)}) collective-permute-start(f32[8,128,128]{2,1,0:T(8,128)S(1)} %get-tuple-element.315), channel_id=1, source_target_pairs={{0,28},{4,0},{8,4},{12,8},{16,12},{20,16},{24,20},{28,24},{1,29},{... | collective-permute-start | bytes 1572872 | tf_op jit(solution)/shard_map/ppermute | solution.py:19
  1280.8 1.0 copy-start.4
  1281.8 25.1 %copy-start.1 = (bf16[128,256]{1,0:T(8,128)(2,1)S(1)}, bf16[128,256]{1,0:T(8,128)(2,1)}, u32[]{:S(2)}) copy-start(bf16[128,256]{1,0:T(8,128)(2,1)} %param.17) | copy-start | bytes 196612
Sparse Core Ops, SparseCore 0:
  9.9 160.1 all-gather.1
  1281.9 24.9 reduce-scatter.1
where the time goes:
time: 1320 us; the launch traced here: 1310 us
  local copies, waits for them, and re-layouts  542 us (41%)
  matrix products  346 us (26%)
  waiting for transfers between devices  278 us (21%)
  loops' own time  106 us (8%)
  other arithmetic  19.6 us (1%)
  between operations  14.2 us (1%)
    gather x32, local copies, waits for them, and re-layouts, one_row(): picked = stacked[block_index]  292 us
    all_gather x1, waiting for transfers between devices, per_device(): full_rows = lax.all_gather(blocks, 'col', axis=1, tiled=True)  162 us
    transpose x16, local copies, waits for them, and re-layouts, place_batch(): jnp.einsum('qby,qabz->qayz', row_pick, placed_z, precision=highest)  147 us
    dot_general x16, matrix products, place_batch(): jnp.einsum('qby,qabz->qayz', row_pick, placed_z, precision=highest)  144 us
    another operation x1, loops' own time, per_device(): square = lax.map(one_row, jnp.arange(rows_dev, dtype=jnp.int32))  105 us
    dot_general x16, matrix products, place_batch(): jnp.einsum('qap,qayz->pyz', plane_pick, placed_y, precision=highest)  90.1 us
    ppermute x1, waiting for transfers between devices, extended_2(): lax.ppermute(tail, axis, [(i, (i + 1) % count) for i in range(count)])  88.1 us
    dot_general x32, matrix products, one_row(): jnp.einsum('kmn,ksnp->smp', left_blocks, picked, preferred_element_type=j...  79.8 us
  transfers between devices with their start and end apart: 6, of which 4 were waited for; matrix products, arithmetic and copies ran while one was open for 2% of the time, Pallas kernels for 0%

commit v1 on v0

v1 whole, which is shorter than its diff:
```python
import functools

import jax
import jax.numpy as jnp
from jax import lax
from jax.experimental import pallas as pl
from jax.experimental.pallas import tpu as pltpu
from jax.sharding import PartitionSpec as P

H = 8
PL = 16
TX = 16
TY = 16
TZ = 16
CHUNK = H
LANES = 128


def across(value, axis, flip):
    peers = lax.axis_size(axis)
    return lax.ppermute(value, axis, [(i, i ^ flip) for i in range(peers)])


def from_behind(value, axis, by):
    peers = lax.axis_size(axis)
    return lax.ppermute(value, axis, [(i, (i + by) % peers) for i in range(peers)])


def between_chips(value, axis):
    peers = lax.axis_size(axis)
    return lax.ppermute(value, axis, [(i, (i + (1 if i % 2 else -1)) % peers) for i in range(peers)])


def after(value, *others):
    return lax.optimization_barrier((value,) + others)[0] if others else value


class Links:
    def __init__(self):
        self.sent = {}

    def send(self, link, value, depth, move):
        sent = self.sent.setdefault(link, [])
        if len(sent) >= depth:
            value = after(value, sent[-depth])
        sent.append(move(value))
        return sent[-1]


def second_hops(firsts, slots, axis, befores):
    peers = lax.axis_size(axis)
    bits = [1 << b for b in range(peers.bit_length() - 1)]
    shares = []
    if len(bits) == 2:
        for come, go, part in ((bits[0], bits[1], 0), (bits[1], bits[0], 1)):
            for first, count, hops in firsts:
                if len(firsts) == 1:
                    first, count = first + part * count // 2, count // 2
                    value = hops[come][first * slots : (first + count) * slots]
                elif (first > 0) == part:
                    value = hops[come]
                else:
                    continue
                value = across(after(value, *befores), axis, go)
                shares.append((come ^ go, first, count, value))
        return shares
    for first, count, hops in firsts:
        held = dict(hops)
        for place, bit in enumerate(bits):
            for distance in sorted(held):
                if distance & bit == 0 and distance >> (place + 1) == 0:
                    held[distance | bit] = across(held[distance], axis, bit)
                    shares.append((distance | bit, first, count, held[distance | bit]))
    return shares


def by_spot(chunk, chunks, core):
    return jnp.where(core == 0, chunk, chunks - 1 - chunk)


def in_spots(values, core):
    chunks = values.reshape((values.shape[0] // CHUNK, CHUNK) + values.shape[1:])
    return jnp.where(core == 0, chunks, chunks[::-1]).reshape(values.shape)


def slot_lookup(pattern, first_row, rows, total_rows, col_place, col_count, slots, core):
    kslots = pattern.shape[1]
    shares = jnp.arange(col_count, dtype=jnp.int32) ^ col_place
    picks = (jnp.arange(col_count, dtype=jnp.int32)[None, :] == shares[:, None]).astype(jnp.int32)
    offsets = (pattern - jnp.arange(total_rows, dtype=jnp.int32)[:, None] + H) % total_rows
    offsets = jnp.concatenate([offsets[total_rows - H :], offsets, offsets[:H]], axis=0)
    offsets = lax.dynamic_slice_in_dim(offsets, first_row, rows + 2 * H, 0)
    by_share = offsets.reshape(rows + 2 * H, 1, col_count, slots)
    offsets = jnp.sum(by_share * picks[None, :, :, None], axis=2).reshape(rows + 2 * H, kslots)
    own = offsets[H : H + rows]
    far = jnp.zeros((rows, kslots, kslots), jnp.int32)
    for w in range(2 * H + 1):
        far = far + jnp.where(own[:, :, None] == w, offsets[w : w + rows][:, None, :], 0)
    wanted = own[:, None, :slots] - own[:, :, None] + H
    matches = (far[:, :, None, :] == wanted[:, :, :, None]).astype(jnp.int32)
    matched = jnp.sum(matches, axis=3)
    slot = jnp.sum(matches * jnp.arange(kslots, dtype=jnp.int32), axis=3)
    line = jnp.arange(rows, dtype=jnp.int32)[:, None] + own
    spot = by_spot(line // CHUNK, rows // CHUNK + 2, core)
    place = (
        (spot[:, :, None] * col_count + slot // slots) * CHUNK + (line % CHUNK)[:, :, None]
    ) * slots + slot % slots
    return jnp.where(matched > 0, place, -1)


def square_kernel(
    first_spot, spots, sources, count, last, col_count, slots, kslots, core, look, planes, lines, turns, blocks, *refs
):
    pieces = refs[:count]
    refs = refs[count:]
    basis_x, basis_yz, slab_in, _, square = refs[:5]
    if last:
        middle, low, high, slab = refs[5:9]
        refs = refs[9:]
    else:
        slab = refs[5]
        refs = refs[6:]
    held, result, tiles, load_sems, store_sems = refs
    span = CHUNK * slots
    bsize = held.shape[-1]
    rows = spots * CHUNK
    spare = first_spot - 1
    all_spots = blocks.shape[0] // span

    def load(index):
        piece, take, share, spot_0, spot_1, first, count = sources[index]
        spot = spot_0 if spot_0 == spot_1 else jnp.where(core[0] == 0, spot_0, spot_1)
        to = held.at[pl.ds((((spot - spare) * col_count + share) * CHUNK + first) * slots, count * slots)]
        if piece is None:
            chunk = jnp.where(core[0] == 0, spot - 1, all_spots - spot)
            come = blocks.at[pl.ds((chunk * CHUNK + take) * slots, count * slots)]
        else:
            come = pieces[piece].at[pl.ds(take * slots, count * slots)]
        return pltpu.make_async_copy(come, to, load_sems.at[index])

    for index in range(len(sources)):
        load(index).start()
    if slab_in is None:
        slab[...] = jnp.zeros_like(slab)
    else:
        slab[...] = slab_in[...]
    tiles[...] = jnp.zeros_like(tiles)
    held[(spots + 2) * col_count * span] = jnp.zeros((bsize, bsize), held.dtype)
    lane = lax.broadcasted_iota(jnp.int32, (2 * PL, LANES), 1)

    def wait_for(spot):
        for index in range(len(sources)):
            if min(sources[index][3:5]) == spot:
                load(index).wait()

    for spot in range(2):
        wait_for(spare + spot)

    def place_tiles(row, spot):
        for s in range(slots):
            task = ((first_spot - 1) * CHUNK + row) * slots + s
            turn = turns[task]
            first = lines[task]
            group = ((lane + (LANES - turn)) & (LANES - 1)) // TZ
            halves = [
                pltpu.roll(
                    tiles[spot, s * 2 * PL : (s + 1) * 2 * PL, h * LANES : (h + 1) * LANES], turn, 1
                )
                for h in range(TY * TZ // LANES)
            ]
            per = LANES // TZ
            for b in range(TY):
                slab[first + b] = slab[first + b] + jnp.where(group == b % per, halves[b // per], 0.0)

    def out_copy(row):
        spot = first_spot - 1 + row // CHUNK
        chunk = jnp.where(core[0] == 0, spot, all_spots - 1 - spot)
        return pltpu.make_async_copy(
            result.at[row], square.at[chunk * CHUNK + row % CHUNK], store_sems.at[row]
        )

    def one_row(row, carry):
        for n in range(spots):

            @pl.when(row == n * CHUNK)
            def _():
                wait_for(spare + n + 2)

        spot = row % 2
        own_first = ((row // CHUNK + 1) * col_count) * span + (row % CHUNK) * slots
        overall = (first_spot - 1) * CHUNK + row

        def left(k):
            return held[own_first + (k // slots) * span + k % slots]

        def right(k, s):
            return held[look[(overall * slots + s) * kslots + k]]

        blocks_out = []
        lhs = jnp.concatenate([left(k) for k in range(kslots)], axis=1)
        for p in range(0, slots, 2):
            rhs = jnp.concatenate(
                [
                    jnp.concatenate([right(k, p), right(k, p + 1)], axis=1)
                    for k in range(kslots)
                ],
                axis=0,
            )
            total = jnp.dot(lhs, rhs, preferred_element_type=jnp.float32)
            blocks_out += [total[:, :bsize], total[:, bsize:]]
        for s in range(slots):
            result[row, s] = blocks_out[s]
        density = jnp.concatenate([block.astype(jnp.bfloat16) for block in blocks_out], axis=1)
        halves = jnp.dot(basis_x[...], density, preferred_element_type=jnp.float32)
        halves = jnp.concatenate([halves, jnp.zeros((2 * PL - TX, slots * bsize), jnp.float32)], axis=0)
        halves = [
            pltpu.roll(
                halves[:, s * bsize : (s + 1) * bsize], planes[overall * slots + s], 0
            ).astype(jnp.bfloat16)
            for s in range(slots)
        ]
        place_tiles(jnp.maximum(row - 1, 0), 1 - spot)
        tiles[spot] = jnp.dot(
            jnp.concatenate(halves, axis=0), basis_yz[...], preferred_element_type=jnp.float32
        )
        out_copy(row).start()
        return carry

    lax.fori_loop(0, rows, one_row, 0)
    place_tiles(rows - 1, (rows - 1) % 2)
    per = LANES // TZ

    def straighten(first, carry):
        edges = []
        for b in range(per):
            y = first * per + b
            line = pltpu.roll(slab[y], LANES - TZ * b, 1) if b else slab[y]
            middle[y] = line[TX // 2 : TX // 2 + PL]
            edges.append((line[: TX // 2], line[TX // 2 + PL :]))
        for b in range(0, per, 2):
            pair = (first * per + b) // 2
            for out, side in ((low, 0), (high, 1)):
                both = jnp.concatenate([edges[b][side], edges[b + 1][side]], axis=0)
                out[pair] = both.astype(out.dtype)
        return carry

    if last:
        lax.fori_loop(0, slab.shape[0] // per, straighten, 0)

    def finish(row, carry):
        out_copy(row).wait()
        return carry

    lax.fori_loop(0, rows, finish, 0)


def square_rows(first_spot, spots, sources, pieces, tables, blocks, bases, carried, last, slots, kslots, col_count):
    rows_all = blocks.shape[0] // slots
    bsize = blocks.shape[-1]
    smem = pl.BlockSpec(memory_space=pltpu.SMEM)
    vmem = pl.BlockSpec(memory_space=pltpu.VMEM)
    anywhere = pl.BlockSpec(memory_space=pl.ANY)
    square_shape = jax.ShapeDtypeStruct((rows_all, slots, bsize, bsize), jnp.float32)
    slab_shape = jax.ShapeDtypeStruct((LANES, 2 * PL, LANES), jnp.float32)
    body = functools.partial(square_kernel, first_spot, spots, sources, len(pieces), last, col_count, slots, kslots)
    inputs = tables + [blocks] + pieces + bases
    specs = [smem] * len(tables) + [anywhere] * (1 + len(pieces)) + [vmem] * len(bases)
    aliases = {}
    if carried is None:

        def kernel(*refs):
            body(*refs[: len(inputs)], None, None, *refs[len(inputs) :])

    else:
        kernel = body
        aliases = {len(inputs) + 1: 0}
        inputs = inputs + [carried[1], carried[0]]
        specs = specs + [vmem, anywhere]
    out_shape, slab = (square_shape, slab_shape), []
    if last:
        rim_shape = jax.ShapeDtypeStruct((LANES // 2, TX, LANES), jnp.bfloat16)
        middle_shape = jax.ShapeDtypeStruct((LANES, PL, LANES), jnp.float32)
        out_shape = (square_shape, middle_shape, rim_shape, rim_shape)
        slab = [pltpu.VMEM(slab_shape.shape, jnp.float32)]
    return pl.pallas_call(
        kernel,
        out_shape=out_shape,
        in_specs=specs,
        out_specs=(anywhere,) + (vmem,) * (len(out_shape) - 1),
        scratch_shapes=slab
        + [
            pltpu.VMEM(((spots + 2) * CHUNK * kslots + 1, bsize, bsize), jnp.bfloat16),
            pltpu.VMEM((spots * CHUNK, slots, bsize, bsize), jnp.float32),
            pltpu.VMEM((2, slots * 2 * PL, TY * TZ), jnp.float32),
            pltpu.SemaphoreType.DMA((len(sources),)),
            pltpu.SemaphoreType.DMA((spots * CHUNK,)),
        ],
        input_output_aliases=aliases,
        compiler_params=pltpu.CompilerParams(vmem_limit_bytes=56 * 1024 * 1024),
        cost_estimate=pl.CostEstimate(
            flops=6 * spots * CHUNK * slots * kslots * bsize**3,
            bytes_accessed=24 * 1024 * 1024,
            transcendentals=0,
        ),
        name="square_and_place",
    )(*inputs)


def per_device(blocks, pattern, anchors, basis_x, basis_yz):
    rows, slots, bsize, _ = blocks.shape
    kslots = pattern.shape[1]
    row_count = lax.axis_size("row")
    col_count = lax.axis_size("col")
    row_place = lax.axis_index("row")
    col_place = lax.axis_index("col")
    core = row_place % 2
    total_rows = rows * row_count
    first_row = row_place * rows
    spots = rows // CHUNK
    flat = blocks.reshape(rows * slots, bsize, bsize)

    def own(spot, first, count):
        chunk = by_spot(spot, spots + 2, core) - 1
        return lax.dynamic_slice_in_dim(flat, (chunk * CHUNK + first) * slots, count * slots, 0)

    links = Links()
    moves = {
        "between": functools.partial(between_chips, axis="row"),
        "inside": functools.partial(across, axis="row", flip=1),
    }
    outer = own(1, 0, CHUNK)
    middle = [flat[n * CHUNK * slots : (n + 1) * CHUNK * slots] for n in range(1, spots - 1)]
    inner = own(spots, 0, CHUNK)
    loads = [(None, 0, 0, spot, spot, 0, CHUNK) for spot in range(1, spots + 1)]
    pieces = []

    def keep(value, take, share, spot_0, spot_1, first, count):
        if not any(value is piece for piece in pieces):
            pieces.append(value)
        index = [value is piece for piece in pieces].index(True)
        loads.append((index, take, share, spot_0, spot_1, first, count))

    bits = [1 << b for b in range(col_count.bit_length() - 1)]

    def hop(parts, befores=(), turns=None):
        hops = [{} for _ in parts]
        for place, bit in enumerate(bits):
            for n in range(len(parts)):
                if turns is None or (n == (place % 2) * (len(parts) - 1)) == turns:
                    hops[n][bit] = across(after(parts[n], *befores), "col", bit)
        return hops

    def shares_of(parts, hops, count, befores=()):
        firsts = [(n * count, count, got) for n, got in enumerate(hops)]
        later = second_hops(firsts, slots, "col", befores)
        shares = [(bit, first, count, got[bit]) for first, count, got in firsts for bit in bits]
        return shares + later, [share[3] for share in later]

    outer_hops = hop([outer])
    shares, done = shares_of([outer], outer_hops, CHUNK)
    over = moves["between"](outer)
    keep(over, 0, 0, 0, 0, 0, CHUNK)
    over = moves["between"](after(jnp.concatenate([share[3] for share in shares], axis=0), over))
    take = 0
    for distance, first, count, value in shares:
        keep(value, 0, distance, 1, 1, first, count)
        keep(over, take, distance, 0, 0, first, count)
        take += count
    leading = hop(middle, done, turns=True)
    trailing = hop(middle, done, turns=False)
    middle_hops = [{**one, **other} for one, other in zip(leading, trailing)]
    shares, done = shares_of(middle, middle_hops, CHUNK)
    for distance, first, count, value in shares:
        chunk = first // CHUNK + 2
        keep(value, 0, distance, chunk, spots + 1 - chunk, 0, CHUNK)
    done = done + [value for one in trailing for value in one.values()]
    inner_hops = hop([inner], done)

    def rows_from(first_spot, carried):
        fits = range(first_spot - 1, first_spot + spots // 2 + 1)
        chosen = [load for load in loads if load[3] in fits and load[4] in fits]
        chosen.sort(key=lambda load: min(load[3:5]))
        used = sorted({load[0] for load in chosen if load[0] is not None})
        sources = [
            (None if load[0] is None else used.index(load[0]),) + load[1:] for load in chosen
        ]
        return square_rows(
            first_spot,
            spots // 2,
            sources,
            [pieces[index] for index in used],
            tables,
            flat,
            bases,
            carried,
            first_spot > 1,
            slots,
            kslots,
            col_count,
        )

    look = slot_lookup(pattern, first_row, rows, total_rows, col_place, col_count, slots, core)
    look = in_spots(jnp.transpose(look, (0, 2, 1)), core).reshape(2, -1)
    span = CHUNK * kslots
    skipped = jnp.arange(2, dtype=jnp.int32)[:, None] * (spots // 2 * span)
    look = jnp.where(look < 0, (spots // 2 + 2) * span, look - skipped).reshape(-1)
    own_anchors = lax.dynamic_slice(anchors, (0, first_row, col_place * slots), (3, rows, slots))
    own_anchors = in_spots(jnp.transpose(own_anchors, (1, 0, 2)), core)
    own_anchors = jnp.transpose(own_anchors, (1, 0, 2)).reshape(3, rows * slots)
    margin = TX // 2
    planes = (own_anchors[0] - row_place * PL + margin) % (PL * row_count)
    lines = own_anchors[1]
    turns = (own_anchors[2] + TZ * own_anchors[1]) % LANES
    tables = [jnp.reshape(core, (1,)), look, planes, lines, turns]
    bases = [basis_x, basis_yz]

    early = rows_from(1, None)
    shares, _ = shares_of([inner], inner_hops, CHUNK, early[1:2])
    for distance, first, count, value in shares:
        keep(value, 0, distance, spots, spots, first, count)
    for distance, first, count, value in [(0, 0, CHUNK, inner)] + shares:
        if distance.bit_count() < 2:
            value = after(value, early[1])
        come = links.send("inside", value, 2, moves["inside"])
        keep(come, 0, distance, spots + 1, spots + 1, first, count)
    square, middle_planes, low, high = rows_from(1 + spots // 2, early)

    wire = jnp.bfloat16
    rims = [from_behind(high, "row", 1), from_behind(low, "row", -1)]
    rims = [rim.reshape(LANES, margin, LANES) for rim in rims]
    folded = middle_planes + jnp.concatenate(rims, axis=1).astype(jnp.float32)
    share = LANES // col_count
    by_share = folded.reshape(col_count, share, PL, LANES)
    total = lax.dynamic_index_in_dim(by_share, col_place, 0, keepdims=False)
    for distance in range(1, col_count):
        sent = lax.dynamic_index_in_dim(by_share, col_place ^ distance, 0, keepdims=False)
        total = total + across(sent.astype(wire), "col", distance).astype(jnp.float32)
    return square, jnp.transpose(total, (1, 0, 2))


def solution(mesh):
    placed = (P("row", "col", None, None), P(), P(), P(), P())
    return jax.shard_map(
        per_device,
        mesh=mesh,
        in_specs=placed,
        out_specs=(P("row", "col", None, None), P("row", "col", None)),
        check_vma=False,
    )
```

time: 1320 us -> 208 us (0.16)
  local copies, waits for them, and re-layouts: 542 us -> 6.99 us
  matrix products: 346 us -> 0 us
  waiting for transfers between devices: 278 us -> 122 us
  loops' own time: 106 us -> 0 us
  Pallas kernels: 0 us -> 40.9 us
  starting transfers between devices: 7.21 us -> 30.4 us
  other arithmetic: 19.6 us -> 6.35 us
  between operations: 14.2 us -> 0.99 us
    dot_general x82 -> x0, matrix products: 346 us -> none  [the longest x16 144 us: place_batch(): jnp.einsum('qby,qabz->qayz', row_pick, placed_z, precision=highest)]
    gather x64 -> x0, local copies, waits for them, and re-layouts: 310 us -> none  [the longest x32 292 us: one_row(): picked = stacked[block_index]]
    all_gather x1 -> x0, waiting for transfers between devices: 162 us -> none  [per_device(): full_rows = lax.all_gather(blocks, 'col', axis=1, tiled=True)]
    transpose x16 -> x1, local copies, waits for them, and re-layouts: 147 us -> 0.08 us  [per_device(): own_anchors = in_spots(jnp.transpose(own_anchors, (1, 0, 2)), core)]
    another operation x2 -> x0, loops' own time: 106 us -> none  [the longest x1 105 us: per_device(): square = lax.map(one_row, jnp.arange(rows_dev, dtype=jnp.int32))]
    pallas_call x0 -> x2, Pallas kernels: none -> 40.9 us  [square_rows(): pl.pallas_call(kernel, out_shape=out_shape, in_specs=specs, out_specs=(an...]
    ppermute x2 -> x24, waiting for transfers between devices: 88.1 us -> 116 us  [the longest x22 116 us: across(): return lax.ppermute(value, axis, [(i, i ^ flip) for i in range(peers)])]
    ppermute x2 -> x24, starting transfers between devices: 3.54 us -> 26.8 us  [the longest x22 23.2 us: across(): return lax.ppermute(value, axis, [(i, i ^ flip) for i in range(peers)])]
  transfers between devices with their start and end apart: 6 -> 26, of which waited for: 4 -> 15; matrix products, arithmetic and copies ran while one was open for 2% -> 3% of each run, Pallas kernels for 0% -> 10%
where the time goes in v1:
time: 208 us
  waiting for transfers between devices  122 us (59%)
  Pallas kernels  40.9 us (20%)
  starting transfers between devices  30.4 us (15%)
  local copies, waits for them, and re-layouts  6.99 us (3%)
  other arithmetic  6.35 us (3%)
    ppermute x22, waiting for transfers between devices, across(): return lax.ppermute(value, axis, [(i, i ^ flip) for i in range(peers)])  116 us
    pallas_call x2, Pallas kernels, square_rows(): pl.pallas_call(kernel, out_shape=out_shape, in_specs=specs, out_specs=(an...  40.9 us
    ppermute x22, starting transfers between devices, across(): return lax.ppermute(value, axis, [(i, i ^ flip) for i in range(peers)])  23.2 us
    ppermute x2, waiting for transfers between devices, from_behind(): lax.ppermute(value, axis, [(i, (i + by) % peers) for i in range(peers)])  6.71 us
  transfers between devices with their start and end apart: 26, of which 15 were waited for; matrix products, arithmetic and copies ran while one was open for 3% of the time, Pallas kernels for 10%

profile of v1, /device:TPU:0, one launch (start us, length us, event | category | flops | bytes accessed | tf_op | source)
XLA Modules:
  0.0 208.1 jit_solution(18068409402117079772)
XLA Ops:
  0.7 3.1 %constant_dynamic-slice_fusion.3 = (bf16[32,128,128]{2,1,0:T(8,128)(2,1)}, bf16[32,128,128]{2,1,0:T(8,128)(2,1)}) fusion(bf16[128,128,128]{2,1,0:T(8,128)(2,1)} %bitcast.79, s32[]{:T(128)S(6)} %select_n.287, s32[]{:T(128)S(6)} %select_n.285), kind=kLoop, calls=%fused_computation.84 | loop fusion | bytes 4194312 | tf_op jit(solution)/shard_map/dynamic_slice | solution.py:324
  3.8 2.9 %collective-permute-start = (bf16[32,128,128]{2,1,0:T(8,128)(2,1)}, bf16[32,128,128]{2,1,0:T(8,128)(2,1)S(1)}, u32[]{:S(2)}, u32[]{:S(2)}) collective-permute-start(bf16[32,128,128]{2,1,0:T(8,128)(2,1)} %get-tuple-element.41), channel_id=1, source_target_pairs={{0,1},{1,0},{2,3},{3,2},{4,5},{5,4},{6,7},{7,6},{8,9},{9,8},{10,11... | collective-permute-start | bytes 3145736 | tf_op jit(solution)/shard_map/ppermute | solution.py:21
  6.7 1.5 collective-permute-start.2
  8.2 2.5 %collective-permute-start.12 = (bf16[32,128,128]{2,1,0:T(8,128)(2,1)}, bf16[32,128,128]{2,1,0:T(8,128)(2,1)}, u32[]{:S(2)}, u32[]{:S(2)}) collective-permute-start(bf16[32,128,128]{2,1,0:T(8,128)(2,1)} %get-tuple-element.41), channel_id=1, source_target_pairs={{0,28},{4,8},{8,4},{12,16},{16,12},{20,24},{24,20},{28,0},{1,29},{... | collective-permute-start | bytes 3145736 | tf_op jit(solution)/shard_map/ppermute | solution.py:31
  11.1 19.0 %collective-permute-done.refs_7_ = bf16[32,128,128]{2,1,0:T(8,128)(2,1)S(1)} collective-permute-done((bf16[32,128,128]{2,1,0:T(8,128)(2,1)}, bf16[32,128,128]{2,1,0:T(8,128)(2,1)S(1)}, u32[]{:S(2)}, u32[]{:S(2)}) %collective-permute-start) | collective-permute-done | bytes 1048608 | tf_op jit(solution)/shard_map/ppermute | solution.py:21
  30.1 1.8 collective-permute-start.1
  32.0 1.6 collective-permute-start.3
  33.7 9.7 %collective-permute-done.1.refs_10_ = bf16[16,128,128]{2,1,0:T(8,128)(2,1)S(1)} collective-permute-done((bf16[16,128,128]{2,1,0:T(8,128)(2,1)S(1)}, bf16[16,128,128]{2,1,0:T(8,128)(2,1)S(1)}, u32[]{:S(2)}, u32[]{:S(2)}) %collective-permute-start.1) | collective-permute-done | bytes 524320 | tf_op jit(solution)/shard_map/ppermute | solution.py:21
  44.7 2.0 pad_maximum_fusion
  48.1 1.6 fusion.29
  54.7 21.2 %collective-permute-done.7.refs_15_.refs_3_ = bf16[32,128,128]{2,1,0:T(8,128)(2,1)} collective-permute-done((bf16[32,128,128]{2,1,0:T(8,128)(2,1)}, bf16[32,128,128]{2,1,0:T(8,128)(2,1)}, u32[]{:S(2)}, u32[]{:S(2)}) %collective-permute-start.7) | collective-permute-done | bytes 1048608 | tf_op jit(solution)/shard_map/ppermute | solution.py:21
  75.9 1.5 collective-permute-start.9
  80.0 19.5 %collective-permute-done.6.refs_14_.refs_2_ = bf16[32,128,128]{2,1,0:T(8,128)(2,1)} collective-permute-done((bf16[32,128,128]{2,1,0:T(8,128)(2,1)}, bf16[32,128,128]{2,1,0:T(8,128)(2,1)}, u32[]{:S(2)}, u32[]{:S(2)}) %collective-permute-start.6) | collective-permute-done | bytes 1048608 | tf_op jit(solution)/shard_map/ppermute | solution.py:21
  99.5 21.9 %collective-permute-done.9.refs_17_.refs_5_ = bf16[32,128,128]{2,1,0:T(8,128)(2,1)} collective-permute-done((bf16[32,128,128]{2,1,0:T(8,128)(2,1)}, bf16[32,128,128]{2,1,0:T(8,128)(2,1)}, u32[]{:S(2)}, u32[]{:S(2)}) %collective-permute-start.9) | collective-permute-done | bytes 1048608 | tf_op jit(solution)/shard_map/ppermute | solution.py:21
  122.4 1.5 collective-permute-start.10
  123.9 20.1 %square_and_place.2 = (f32[32,4,128,128]{3,2,1,0:T(8,128)}, f32[128,32,128]{2,1,0:T(8,128)}) custom-call(s32[1]{0:T(128)} %bitcast.refs_0_.core, s32[2048]{0:T(1024)} %fusion.22.refs_1_.look, s32[128]{0:T(128)} %get-tuple-element.89.refs_2_.planes, s32[128]{0:T(128)} %copy-done.10, s32[128]{0:T(128)} %get-tuple-element.88.refs_4_.turns, ...), custom_call_target="tpu_custom_call" | custom-call | flops 12884901888 | bytes 25165824 | tf_op jit(solution)/shard_map/square_and_place/pallas_call | solution.py:285
  144.1 2.2 %collective-permute-done.11.refs_7_ = bf16[32,128,128]{2,1,0:T(8,128)(2,1)S(1)} collective-permute-done((bf16[32,128,128]{2,1,0:T(8,128)(2,1)}, bf16[32,128,128]{2,1,0:T(8,128)(2,1)S(1)}, u32[]{:S(2)}, u32[]{:S(2)}) %collective-permute-start.11) | collective-permute-done | bytes 1048608 | tf_op jit(solution)/shard_map/ppermute | solution.py:21
  149.7 11.7 %collective-permute-done.14.refs_8_ = bf16[16,128,128]{2,1,0:T(8,128)(2,1)S(1)} collective-permute-done((bf16[16,128,128]{2,1,0:T(8,128)(2,1)S(1)}, bf16[16,128,128]{2,1,0:T(8,128)(2,1)S(1)}, u32[]{:S(2)}, u32[]{:S(2)}) %collective-permute-start.14) | collective-permute-done | bytes 524320 | tf_op jit(solution)/shard_map/ppermute | solution.py:21
  165.1 20.8 %square_and_place.3 = (f32[32,4,128,128]{3,2,1,0:T(8,128)}, f32[128,16,128]{2,1,0:T(8,128)}, bf16[64,16,128]{2,1,0:T(8,128)(2,1)}, bf16[64,16,128]{2,1,0:T(8,128)(2,1)}) custom-call(s32[1]{0:T(128)} %bitcast.refs_0_.core, s32[2048]{0:T(1024)} %fusion.22.refs_1_.look, s32[128]{0:T(128)} %get-tuple-element.89.refs_2_.planes, ...), custom_call_target="tpu_custom_call", output_to_operand_aliasing={{0}: (24, {})} | custom-call | flops 12884901888 | bytes 25165824 | tf_op jit(solution)/shard_map/square_and_place/pallas_call | solution.py:285
  186.1 3.4 %collective-permute-start.22 = (bf16[64,16,128]{2,1,0:T(8,128)(2,1)}, bf16[64,16,128]{2,1,0:T(8,128)(2,1)S(1)}, u32[]{:S(2)}, u32[]{:S(2)}) collective-permute-start(bf16[64,16,128]{2,1,0:T(8,128)(2,1)} %get-tuple-element.37), channel_id=1, source_target_pairs={{0,28},{4,0},{8,4},{12,8},{16,12},{20,16},{24,20},{28,24},{1,29},{... | collective-permute-start | bytes 786440 | tf_op jit(solution)/shard_map/ppermute | solution.py:26
  189.5 6.7 %collective-permute-done.21 = bf16[64,16,128]{2,1,0:T(8,128)(2,1)S(1)} collective-permute-done((bf16[64,16,128]{2,1,0:T(8,128)(2,1)}, bf16[64,16,128]{2,1,0:T(8,128)(2,1)S(1)}, u32[]{:S(2)}, u32[]{:S(2)}) %collective-permute-start.21) | collective-permute-done | bytes 262176 | tf_op jit(solution)/shard_map/ppermute | solution.py:26
  197.7 1.4 collective-permute-start.23
  201.5 2.1 %collective-permute-done.23 = bf16[32,16,128]{2,0,1:T(8,128)(2,1)S(1)} collective-permute-done((bf16[32,16,128]{2,0,1:T(8,128)(2,1)S(1)}, bf16[32,16,128]{2,0,1:T(8,128)(2,1)S(1)}, u32[]{:S(2)}, u32[]{:S(2)}) %collective-permute-start.23) | collective-permute-done | bytes 131104 | tf_op jit(solution)/shard_map/ppermute | solution.py:21
  203.6 3.7 %collective-permute-done.24 = bf16[32,16,128]{2,0,1:T(8,128)(2,1)S(1)} collective-permute-done((bf16[32,16,128]{2,0,1:T(8,128)(2,1)S(1)}, bf16[32,16,128]{2,0,1:T(8,128)(2,1)S(1)}, u32[]{:S(2)}, u32[]{:S(2)}) %collective-permute-start.24) | collective-permute-done | bytes 131104 | tf_op jit(solution)/shard_map/ppermute | solution.py:21
  (111 shorter events, 23.7 us)
Async XLA Ops:
  3.8 26.3 %collective-permute-start = (bf16[32,128,128]{2,1,0:T(8,128)(2,1)}, bf16[32,128,128]{2,1,0:T(8,128)(2,1)S(1)}, u32[]{:S(2)}, u32[]{:S(2)}) collective-permute-start(bf16[32,128,128]{2,1,0:T(8,128)(2,1)} %get-tuple-element.41), channel_id=1, source_target_pairs={{0,1},{1,0},{2,3},{3,2},{4,5},{5,4},{6,7},{7,6},{8,9},{9,8},{10,11... | collective-permute-start | bytes 3145736 | tf_op jit(solution)/shard_map/ppermute | solution.py:21
  6.7 25.3 %collective-permute-start.2 = (bf16[32,128,128]{2,1,0:T(8,128)(2,1)}, bf16[32,128,128]{2,1,0:T(8,128)(2,1)S(1)}, u32[]{:S(2)}, u32[]{:S(2)}) collective-permute-start(bf16[32,128,128]{2,1,0:T(8,128)(2,1)} %get-tuple-element.41), channel_id=1, source_target_pairs={{0,2},{1,3},{2,0},{3,1},{4,6},{5,7},{6,4},{7,5},{8,10},{9,11},{10,... | collective-permute-start | bytes 3145736 | tf_op jit(solution)/shard_map/ppermute | solution.py:21
  8.2 38.5 %collective-permute-start.12 = (bf16[32,128,128]{2,1,0:T(8,128)(2,1)}, bf16[32,128,128]{2,1,0:T(8,128)(2,1)}, u32[]{:S(2)}, u32[]{:S(2)}) collective-permute-start(bf16[32,128,128]{2,1,0:T(8,128)(2,1)} %get-tuple-element.41), channel_id=1, source_target_pairs={{0,28},{4,8},{8,4},{12,16},{16,12},{20,24},{24,20},{28,0},{1,29},{... | collective-permute-start | bytes 3145736 | tf_op jit(solution)/shard_map/ppermute | solution.py:31
  30.1 13.3 %collective-permute-start.1 = (bf16[16,128,128]{2,1,0:T(8,128)(2,1)S(1)}, bf16[16,128,128]{2,1,0:T(8,128)(2,1)S(1)}, u32[]{:S(2)}, u32[]{:S(2)}) collective-permute-start(bf16[16,128,128]{2,1,0:T(8,128)(2,1)S(1)} %slice.169), channel_id=1, source_target_pairs={{0,2},{1,3},{2,0},{3,1},{4,6},{5,7},{6,4},{7,5},{8,10},{9,11},{10,... | collective-permute-start | bytes 1572872 | tf_op jit(solution)/shard_map/ppermute | solution.py:21
  32.0 12.7 %collective-permute-start.3 = (bf16[16,128,128]{2,1,0:T(8,128)(2,1)S(1)}, bf16[16,128,128]{2,1,0:T(8,128)(2,1)S(1)}, u32[]{:S(2)}, u32[]{:S(2)}) collective-permute-start(bf16[16,128,128]{2,1,0:T(8,128)(2,1)S(1)} %slice.170), channel_id=1, source_target_pairs={{0,1},{1,0},{2,3},{3,2},{4,5},{5,4},{6,7},{7,6},{8,9},{9,8},{10,11... | collective-permute-start | bytes 1572872 | tf_op jit(solution)/shard_map/ppermute | solution.py:21
  46.7 77.1 %collective-permute-start.13 = (bf16[96,128,128]{2,1,0:T(8,128)(2,1)S(1)}, bf16[96,128,128]{2,1,0:T(8,128)(2,1)}, u32[]{:S(2)}, u32[]{:S(2)}) collective-permute-start(bf16[96,128,128]{2,1,0:T(8,128)(2,1)S(1)} %pad_maximum_fusion), channel_id=1, source_target_pairs={{0,28},{4,8},{8,4},{12,16},{16,12},{20,24},{24,20},{28,0},{1,29},{... | collective-permute-start | bytes 9437192 | tf_op jit(solution)/shard_map/ppermute | solution.py:31
  49.7 26.3 %collective-permute-start.7 = (bf16[32,128,128]{2,1,0:T(8,128)(2,1)}, bf16[32,128,128]{2,1,0:T(8,128)(2,1)}, u32[]{:S(2)}, u32[]{:S(2)}) collective-permute-start(bf16[32,128,128]{2,1,0:T(8,128)(2,1)} %bitcast.28), channel_id=1, source_target_pairs={{0,2},{1,3},{2,0},{3,1},{4,6},{5,7},{6,4},{7,5},{8,10},{9,11},{10,... | collective-permute-start | bytes 3145736 | tf_op jit(solution)/shard_map/ppermute | solution.py:21
  50.7 26.7 %collective-permute-start.4 = (bf16[32,128,128]{2,1,0:T(8,128)(2,1)}, bf16[32,128,128]{2,1,0:T(8,128)(2,1)}, u32[]{:S(2)}, u32[]{:S(2)}) collective-permute-start(bf16[32,128,128]{2,1,0:T(8,128)(2,1)} %bitcast.27), channel_id=1, source_target_pairs={{0,1},{1,0},{2,3},{3,2},{4,5},{5,4},{6,7},{7,6},{8,9},{9,8},{10,11... | collective-permute-start | bytes 3145736 | tf_op jit(solution)/shard_map/ppermute | solution.py:21
  52.8 46.7 %collective-permute-start.6 = (bf16[32,128,128]{2,1,0:T(8,128)(2,1)}, bf16[32,128,128]{2,1,0:T(8,128)(2,1)}, u32[]{:S(2)}, u32[]{:S(2)}) collective-permute-start(bf16[32,128,128]{2,1,0:T(8,128)(2,1)} %bitcast.28), channel_id=1, source_target_pairs={{0,1},{1,0},{2,3},{3,2},{4,5},{5,4},{6,7},{7,6},{8,9},{9,8},{10,11... | collective-permute-start | bytes 3145736 | tf_op jit(solution)/shard_map/ppermute | solution.py:21
  53.7 45.7 %collective-permute-start.5 = (bf16[32,128,128]{2,1,0:T(8,128)(2,1)}, bf16[32,128,128]{2,1,0:T(8,128)(2,1)}, u32[]{:S(2)}, u32[]{:S(2)}) collective-permute-start(bf16[32,128,128]{2,1,0:T(8,128)(2,1)} %bitcast.27), channel_id=1, source_target_pairs={{0,2},{1,3},{2,0},{3,1},{4,6},{5,7},{6,4},{7,5},{8,10},{9,11},{10,... | collective-permute-start | bytes 3145736 | tf_op jit(solution)/shard_map/ppermute | solution.py:21
  75.9 45.5 %collective-permute-start.9 = (bf16[32,128,128]{2,1,0:T(8,128)(2,1)}, bf16[32,128,128]{2,1,0:T(8,128)(2,1)}, u32[]{:S(2)}, u32[]{:S(2)}) collective-permute-start(bf16[32,128,128]{2,1,0:T(8,128)(2,1)} %collective-permute-done.7.refs_15_.refs_3_), channel_id=1, source_target_pairs={{0,1},{1,0},{2,3},{3,2},{4,5},{5,4},{6,7},{7,6},{8,9},{9,8},{10,11... | collective-permute-start | bytes 3145736 | tf_op jit(solution)/shard_map/ppermute | solution.py:21
  77.4 44.0 %collective-permute-start.8 = (bf16[32,128,128]{2,1,0:T(8,128)(2,1)}, bf16[32,128,128]{2,1,0:T(8,128)(2,1)}, u32[]{:S(2)}, u32[]{:S(2)}) collective-permute-start(bf16[32,128,128]{2,1,0:T(8,128)(2,1)} %collective-permute-done.4.refs_12_.refs_0_), channel_id=1, source_target_pairs={{0,2},{1,3},{2,0},{3,1},{4,6},{5,7},{6,4},{7,5},{8,10},{9,11},{10,... | collective-permute-start | bytes 3145736 | tf_op jit(solution)/shard_map/ppermute | solution.py:21
  121.4 24.8 %collective-permute-start.11 = (bf16[32,128,128]{2,1,0:T(8,128)(2,1)}, bf16[32,128,128]{2,1,0:T(8,128)(2,1)S(1)}, u32[]{:S(2)}, u32[]{:S(2)}) collective-permute-start(bf16[32,128,128]{2,1,0:T(8,128)(2,1)} %get-tuple-element.27), channel_id=1, source_target_pairs={{0,2},{1,3},{2,0},{3,1},{4,6},{5,7},{6,4},{7,5},{8,10},{9,11},{10,... | collective-permute-start | bytes 3145736 | tf_op jit(solution)/shard_map/ppermute | solution.py:21
  122.4 24.5 %collective-permute-start.10 = (bf16[32,128,128]{2,1,0:T(8,128)(2,1)}, bf16[32,128,128]{2,1,0:T(8,128)(2,1)S(1)}, u32[]{:S(2)}, u32[]{:S(2)}) collective-permute-start(bf16[32,128,128]{2,1,0:T(8,128)(2,1)} %get-tuple-element.27), channel_id=1, source_target_pairs={{0,1},{1,0},{2,3},{3,2},{4,5},{5,4},{6,7},{7,6},{8,9},{9,8},{10,11... | collective-permute-start | bytes 3145736 | tf_op jit(solution)/shard_map/ppermute | solution.py:21
  144.0 2.9 %collective-permute-start.16 = (bf16[32,128,128]{2,1,0:T(8,128)(2,1)S(1)}, bf16[32,128,128]{2,1,0:T(8,128)(2,1)S(1)}, u32[]{:S(2)}, u32[]{:S(2)}) collective-permute-start(bf16[32,128,128]{2,1,0:T(8,128)(2,1)S(1)} %copy-done.4), channel_id=1, source_target_pairs={{0,4},{4,0},{8,12},{12,8},{16,20},{20,16},{24,28},{28,24},{1,5},{5... | collective-permute-start | bytes 3145736 | tf_op jit(solution)/shard_map/ppermute | solution.py:21
  146.9 14.5 %collective-permute-start.17 = (bf16[32,128,128]{2,1,0:T(8,128)(2,1)S(1)}, bf16[32,128,128]{2,1,0:T(8,128)(2,1)S(1)}, u32[]{:S(2)}, u32[]{:S(2)}) collective-permute-start(bf16[32,128,128]{2,1,0:T(8,128)(2,1)S(1)} %collective-permute-done.10.refs_6_), channel_id=1, source_target_pairs={{0,4},{4,0},{8,12},{12,8},{16,20},{20,16},{24,28},{28,24},{1,5},{5... | collective-permute-start | bytes 3145736 | tf_op jit(solution)/shard_map/ppermute | solution.py:21
  146.9 15.4 %collective-permute-start.18 = (bf16[32,128,128]{2,1,0:T(8,128)(2,1)S(1)}, bf16[32,128,128]{2,1,0:T(8,128)(2,1)S(1)}, u32[]{:S(2)}, u32[]{:S(2)}) collective-permute-start(bf16[32,128,128]{2,1,0:T(8,128)(2,1)S(1)} %collective-permute-done.11.refs_7_), channel_id=1, source_target_pairs={{0,4},{4,0},{8,12},{12,8},{16,20},{20,16},{24,28},{28,24},{1,5},{5... | collective-permute-start | bytes 3145736 | tf_op jit(solution)/shard_map/ppermute | solution.py:21
  147.5 14.0 %collective-permute-start.14 = (bf16[16,128,128]{2,1,0:T(8,128)(2,1)S(1)}, bf16[16,128,128]{2,1,0:T(8,128)(2,1)S(1)}, u32[]{:S(2)}, u32[]{:S(2)}) collective-permute-start(bf16[16,128,128]{2,1,0:T(8,128)(2,1)S(1)} %slice.171), channel_id=1, source_target_pairs={{0,2},{1,3},{2,0},{3,1},{4,6},{5,7},{6,4},{7,5},{8,10},{9,11},{10,... | collective-permute-start | bytes 1572872 | tf_op jit(solution)/shard_map/ppermute | solution.py:21
  148.6 13.7 %collective-permute-start.15 = (bf16[16,128,128]{2,1,0:T(8,128)(2,1)S(1)}, bf16[16,128,128]{2,1,0:T(8,128)(2,1)S(1)}, u32[]{:S(2)}, u32[]{:S(2)}) collective-permute-start(bf16[16,128,128]{2,1,0:T(8,128)(2,1)S(1)} %slice.172), channel_id=1, source_target_pairs={{0,1},{1,0},{2,3},{3,2},{4,5},{5,4},{6,7},{7,6},{8,9},{9,8},{10,11... | collective-permute-start | bytes 1572872 | tf_op jit(solution)/shard_map/ppermute | solution.py:21
  185.9 10.3 %collective-permute-start.21 = (bf16[64,16,128]{2,1,0:T(8,128)(2,1)}, bf16[64,16,128]{2,1,0:T(8,128)(2,1)S(1)}, u32[]{:S(2)}, u32[]{:S(2)}) collective-permute-start(bf16[64,16,128]{2,1,0:T(8,128)(2,1)} %get-tuple-element.36), channel_id=1, source_target_pairs={{0,4},{4,8},{8,12},{12,16},{16,20},{20,24},{24,28},{28,0},{1,5},{5... | collective-permute-start | bytes 786440 | tf_op jit(solution)/shard_map/ppermute | solution.py:26
  186.1 10.1 %collective-permute-start.22 = (bf16[64,16,128]{2,1,0:T(8,128)(2,1)}, bf16[64,16,128]{2,1,0:T(8,128)(2,1)S(1)}, u32[]{:S(2)}, u32[]{:S(2)}) collective-permute-start(bf16[64,16,128]{2,1,0:T(8,128)(2,1)} %get-tuple-element.37), channel_id=1, source_target_pairs={{0,28},{4,0},{8,4},{12,8},{16,12},{20,16},{24,20},{28,24},{1,29},{... | collective-permute-start | bytes 786440 | tf_op jit(solution)/shard_map/ppermute | solution.py:26
  197.7 5.9 %collective-permute-start.23 = (bf16[32,16,128]{2,0,1:T(8,128)(2,1)S(1)}, bf16[32,16,128]{2,0,1:T(8,128)(2,1)S(1)}, u32[]{:S(2)}, u32[]{:S(2)}) collective-permute-start(bf16[32,16,128]{2,0,1:T(8,128)(2,1)S(1)} %bitcast.94), channel_id=1, source_target_pairs={{0,1},{1,0},{2,3},{3,2},{4,5},{5,4},{6,7},{7,6},{8,9},{9,8},{10,11... | collective-permute-start | bytes 393224 | tf_op jit(solution)/shard_map/ppermute | solution.py:21
  199.1 8.1 %collective-permute-start.24 = (bf16[32,16,128]{2,0,1:T(8,128)(2,1)S(1)}, bf16[32,16,128]{2,0,1:T(8,128)(2,1)S(1)}, u32[]{:S(2)}, u32[]{:S(2)}) collective-permute-start(bf16[32,16,128]{2,0,1:T(8,128)(2,1)S(1)} %bitcast.95), channel_id=1, source_target_pairs={{0,2},{1,3},{2,0},{3,1},{4,6},{5,7},{6,4},{7,5},{8,10},{9,11},{10,... | collective-permute-start | bytes 393224 | tf_op jit(solution)/shard_map/ppermute | solution.py:21
  200.3 6.9 %collective-permute-start.25 = (bf16[32,16,128]{2,0,1:T(8,128)(2,1)S(1)}, bf16[32,16,128]{2,0,1:T(8,128)(2,1)S(1)}, u32[]{:S(2)}, u32[]{:S(2)}) collective-permute-start(bf16[32,16,128]{2,0,1:T(8,128)(2,1)S(1)} %bitcast.96), channel_id=1, source_target_pairs={{0,3},{1,2},{2,1},{3,0},{4,7},{5,6},{6,5},{7,4},{8,11},{9,10},{10,... | collective-permute-start | bytes 393224 | tf_op jit(solution)/shard_map/ppermute | solution.py:21
  (20 other events, 198.8 us)

commit v2 on v1

--- a/solution.py
+++ b/solution.py
@@ -13,6 +13,7 @@
 TY = 16
 TZ = 16
 CHUNK = H
+ROWS = 4
 LANES = 128
 
 
@@ -35,19 +36,7 @@
     return lax.optimization_barrier((value,) + others)[0] if others else value
 
 
-class Links:
-    def __init__(self):
-        self.sent = {}
-
-    def send(self, link, value, depth, move):
-        sent = self.sent.setdefault(link, [])
-        if len(sent) >= depth:
-            value = after(value, sent[-depth])
-        sent.append(move(value))
-        return sent[-1]
-
-
-def second_hops(firsts, slots, axis, befores):
+def second_hops(firsts, slots, axis, befores, cut=None):
     peers = lax.axis_size(axis)
     bits = [1 << b for b in range(peers.bit_length() - 1)]
     shares = []
@@ -61,8 +50,10 @@
                     value = hops[come]
                 else:
                     continue
-                value = across(after(value, *befores), axis, go)
-                shares.append((come ^ go, first, count, value))
+                for take in range(0, count, cut or count):
+                    some = value[take * slots : (take + (cut or count)) * slots]
+                    some = across(after(some, *befores), axis, go)
+                    shares.append((come ^ go, first + take, cut or count, some))
         return shares
     for first, count, hops in firsts:
         held = dict(hops)
@@ -115,19 +106,19 @@
     refs = refs[count:]
     basis_x, basis_yz, slab_in, _, square = refs[:5]
     if last:
-        middle, low, high, slab = refs[5:9]
-        refs = refs[9:]
+        middle, low, high, slab, before, before_sem = refs[5:11]
+        refs = refs[11:]
     else:
         slab = refs[5]
         refs = refs[6:]
-    held, result, tiles, load_sems, store_sems = refs
+    held, result, density, tiles, load_sems, store_sems = refs
     span = CHUNK * slots
     bsize = held.shape[-1]
     rows = spots * CHUNK
     spare = first_spot - 1
     all_spots = blocks.shape[0] // span
 
-    def load(index):
+    def load(index, which=0):
         piece, take, share, spot_0, spot_1, first, count = sources[index]
         spot = spot_0 if spot_0 == spot_1 else jnp.where(core[0] == 0, spot_0, spot_1)
         to = held.at[pl.ds((((spot - spare) * col_count + share) * CHUNK + first) * slots, count * slots)]
@@ -135,16 +126,31 @@
             chunk = jnp.where(core[0] == 0, spot - 1, all_spots - spot)
             come = blocks.at[pl.ds((chunk * CHUNK + take) * slots, count * slots)]
         else:
+            if isinstance(piece, tuple):
+                piece, take = piece[which], take[which]
             come = pieces[piece].at[pl.ds(take * slots, count * slots)]
         return pltpu.make_async_copy(come, to, load_sems.at[index])
 
+    def start(index, which):
+        @pl.when(core[0] == which)
+        def _():
+            load(index, which).start()
+
     for index in range(len(sources)):
-        load(index).start()
-    if slab_in is None:
+        if isinstance(sources[index][0], tuple):
+            for which in range(2):
+                start(index, which)
+        else:
+            load(index).start()
+    if last:
+        earlier = pltpu.make_async_copy(slab_in, before, before_sem)
+        earlier.start()
+    if last or slab_in is None:
         slab[...] = jnp.zeros_like(slab)
     else:
         slab[...] = slab_in[...]
     tiles[...] = jnp.zeros_like(tiles)
+    density[...] = jnp.zeros_like(density)
     held[(spots + 2) * col_count * span] = jnp.zeros((bsize, bsize), held.dtype)
     lane = lax.broadcasted_iota(jnp.int32, (2 * PL, LANES), 1)
 
@@ -156,7 +162,10 @@
     for spot in range(2):
         wait_for(spare + spot)
 
-    def place_tiles(row, spot):
+    per = LANES // TZ
+
+    def place(row, turn_of):
+        row = jnp.maximum(row, 0)
         for s in range(slots):
             task = ((first_spot - 1) * CHUNK + row) * slots + s
             turn = turns[task]
@@ -164,54 +173,16 @@
             group = ((lane + (LANES - turn)) & (LANES - 1)) // TZ
             halves = [
                 pltpu.roll(
-                    tiles[spot, s * 2 * PL : (s + 1) * 2 * PL, h * LANES : (h + 1) * LANES], turn, 1
+                    tiles[turn_of, s * 2 * PL : (s + 1) * 2 * PL, h * LANES : (h + 1) * LANES], turn, 1
                 )
                 for h in range(TY * TZ // LANES)
             ]
-            per = LANES // TZ
             for b in range(TY):
                 slab[first + b] = slab[first + b] + jnp.where(group == b % per, halves[b // per], 0.0)
 
-    def out_copy(row):
-        spot = first_spot - 1 + row // CHUNK
-        chunk = jnp.where(core[0] == 0, spot, all_spots - 1 - spot)
-        return pltpu.make_async_copy(
-            result.at[row], square.at[chunk * CHUNK + row % CHUNK], store_sems.at[row]
-        )
-
-    def one_row(row, carry):
-        for n in range(spots):
-
-            @pl.when(row == n * CHUNK)
-            def _():
-                wait_for(spare + n + 2)
-
-        spot = row % 2
-        own_first = ((row // CHUNK + 1) * col_count) * span + (row % CHUNK) * slots
-        overall = (first_spot - 1) * CHUNK + row
-
-        def left(k):
-            return held[own_first + (k // slots) * span + k % slots]
-
-        def right(k, s):
-            return held[look[(overall * slots + s) * kslots + k]]
-
-        blocks_out = []
-        lhs = jnp.concatenate([left(k) for k in range(kslots)], axis=1)
-        for p in range(0, slots, 2):
-            rhs = jnp.concatenate(
-                [
-                    jnp.concatenate([right(k, p), right(k, p + 1)], axis=1)
-                    for k in range(kslots)
-                ],
-                axis=0,
-            )
-            total = jnp.dot(lhs, rhs, preferred_element_type=jnp.float32)
-            blocks_out += [total[:, :bsize], total[:, bsize:]]
-        for s in range(slots):
-            result[row, s] = blocks_out[s]
-        density = jnp.concatenate([block.astype(jnp.bfloat16) for block in blocks_out], axis=1)
-        halves = jnp.dot(basis_x[...], density, preferred_element_type=jnp.float32)
+    def spread(row, turn_of):
+        overall = (first_spot - 1) * CHUNK + jnp.maximum(row, 0)
+        halves = jnp.dot(basis_x[...], density[turn_of], preferred_element_type=jnp.float32)
         halves = jnp.concatenate([halves, jnp.zeros((2 * PL - TX, slots * bsize), jnp.float32)], axis=0)
         halves = [
             pltpu.roll(
@@ -219,22 +190,68 @@
             ).astype(jnp.bfloat16)
             for s in range(slots)
         ]
-        place_tiles(jnp.maximum(row - 1, 0), 1 - spot)
-        tiles[spot] = jnp.dot(
+        tiles[turn_of] = jnp.dot(
             jnp.concatenate(halves, axis=0), basis_yz[...], preferred_element_type=jnp.float32
         )
+
+    def out_copy(row):
+        spot = first_spot - 1 + row // CHUNK
+        chunk = jnp.where(core[0] == 0, spot, all_spots - 1 - spot)
+        return pltpu.make_async_copy(
+            result.at[row], square.at[chunk * CHUNK + row % CHUNK], store_sems.at[row]
+        )
+
+    def product(row, turn_of):
+        own_first = ((row // CHUNK + 1) * col_count) * span + (row % CHUNK) * slots
+        overall = (first_spot - 1) * CHUNK + row
+
+        def left(k):
+            return held[own_first + (k // slots) * span + k % slots]
+
+        def right(k, s):
+            return held[look[(overall * slots + s) * kslots + k]]
+
+        lhs = jnp.concatenate([left(k) for k in range(kslots)], axis=1)
+        rhs = jnp.concatenate(
+            [
+                jnp.concatenate([right(k, s) for s in range(slots)], axis=1)
+                for k in range(kslots)
+            ],
+            axis=0,
+        )
+        total = jnp.dot(lhs, rhs, preferred_element_type=jnp.float32)
+        for s in range(slots):
+            result[row, s] = total[:, s * bsize : (s + 1) * bsize]
+        density[turn_of] = total.astype(density.dtype)
         out_copy(row).start()
+
+    steps = CHUNK // ROWS
+
+    def some_rows(step, carry):
+        for n in range(spots):
+
+            @pl.when(step == n * steps)
+            def _():
+                wait_for(spare + 2 + n)
+
+        for r in range(ROWS):
+            row = step * ROWS + r
+            place(row - 2, r % 2)
+            spread(row - 1, 1 - r % 2)
+            product(row, r % 2)
         return carry
 
-    lax.fori_loop(0, rows, one_row, 0)
-    place_tiles(rows - 1, (rows - 1) % 2)
-    per = LANES // TZ
+    lax.fori_loop(0, rows // ROWS, some_rows, 0)
+    place(rows - 2, 0)
+    spread(rows - 1, 1)
+    place(rows - 1, 1)
 
     def straighten(first, carry):
         edges = []
         for b in range(per):
             y = first * per + b
-            line = pltpu.roll(slab[y], LANES - TZ * b, 1) if b else slab[y]
+            line = slab[y] + before[y]
+            line = pltpu.roll(line, LANES - TZ * b, 1) if b else line
             middle[y] = line[TX // 2 : TX // 2 + PL]
             edges.append((line[: TX // 2], line[TX // 2 + PL :]))
         for b in range(0, per, 2):
@@ -245,6 +262,7 @@
         return carry
 
     if last:
+        earlier.wait()
         lax.fori_loop(0, slab.shape[0] // per, straighten, 0)
 
     def finish(row, carry):
@@ -275,13 +293,13 @@
         kernel = body
         aliases = {len(inputs) + 1: 0}
         inputs = inputs + [carried[1], carried[0]]
-        specs = specs + [vmem, anywhere]
+        specs = specs + [anywhere if last else vmem, anywhere]
     out_shape, slab = (square_shape, slab_shape), []
     if last:
         rim_shape = jax.ShapeDtypeStruct((LANES // 2, TX, LANES), jnp.bfloat16)
         middle_shape = jax.ShapeDtypeStruct((LANES, PL, LANES), jnp.float32)
         out_shape = (square_shape, middle_shape, rim_shape, rim_shape)
-        slab = [pltpu.VMEM(slab_shape.shape, jnp.float32)]
+        slab = [pltpu.VMEM(slab_shape.shape, jnp.float32)] * 2 + [pltpu.SemaphoreType.DMA]
     return pl.pallas_call(
         kernel,
         out_shape=out_shape,
@@ -291,12 +309,13 @@
         + [
             pltpu.VMEM(((spots + 2) * CHUNK * kslots + 1, bsize, bsize), jnp.bfloat16),
             pltpu.VMEM((spots * CHUNK, slots, bsize, bsize), jnp.float32),
+            pltpu.VMEM((2, bsize, slots * bsize), jnp.bfloat16),
             pltpu.VMEM((2, slots * 2 * PL, TY * TZ), jnp.float32),
             pltpu.SemaphoreType.DMA((len(sources),)),
             pltpu.SemaphoreType.DMA((spots * CHUNK,)),
         ],
         input_output_aliases=aliases,
-        compiler_params=pltpu.CompilerParams(vmem_limit_bytes=56 * 1024 * 1024),
+        compiler_params=pltpu.CompilerParams(vmem_limit_bytes=29 * 1024 * 1024),
         cost_estimate=pl.CostEstimate(
             flops=6 * spots * CHUNK * slots * kslots * bsize**3,
             bytes_accessed=24 * 1024 * 1024,
@@ -319,18 +338,18 @@
     spots = rows // CHUNK
     flat = blocks.reshape(rows * slots, bsize, bsize)
 
-    def own(spot, first, count):
+    def own(spot, first, count, befores=()):
         chunk = by_spot(spot, spots + 2, core) - 1
-        return lax.dynamic_slice_in_dim(flat, (chunk * CHUNK + first) * slots, count * slots, 0)
-
-    links = Links()
+        take = after((chunk * CHUNK + first) * slots, *befores)
+        return lax.dynamic_slice_in_dim(flat, take, count * slots, 0)
+
     moves = {
         "between": functools.partial(between_chips, axis="row"),
         "inside": functools.partial(across, axis="row", flip=1),
     }
-    outer = own(1, 0, CHUNK)
+    edge = CHUNK * slots
+    outer = jnp.where(core == 0, flat[:edge], flat[rows * slots - edge :])
     middle = [flat[n * CHUNK * slots : (n + 1) * CHUNK * slots] for n in range(1, spots - 1)]
-    inner = own(spots, 0, CHUNK)
     loads = [(None, 0, 0, spot, spot, 0, CHUNK) for spot in range(1, spots + 1)]
     pieces = []
 
@@ -350,14 +369,15 @@
                     hops[n][bit] = across(after(parts[n], *befores), "col", bit)
         return hops
 
-    def shares_of(parts, hops, count, befores=()):
+    def shares_of(parts, hops, count, befores=(), cut=None):
         firsts = [(n * count, count, got) for n, got in enumerate(hops)]
-        later = second_hops(firsts, slots, "col", befores)
+        later = second_hops(firsts, slots, "col", befores, cut)
         shares = [(bit, first, count, got[bit]) for first, count, got in firsts for bit in bits]
         return shares + later, [share[3] for share in later]
 
     outer_hops = hop([outer])
     shares, done = shares_of([outer], outer_hops, CHUNK)
+    inner = own(spots, 0, CHUNK, done)
     over = moves["between"](outer)
     keep(over, 0, 0, 0, 0, 0, CHUNK)
     over = moves["between"](after(jnp.concatenate([share[3] for share in shares], axis=0), over))
@@ -369,41 +389,68 @@
     leading = hop(middle, done, turns=True)
     trailing = hop(middle, done, turns=False)
     middle_hops = [{**one, **other} for one, other in zip(leading, trailing)]
-    shares, done = shares_of(middle, middle_hops, CHUNK)
+    shares, _ = shares_of(middle, middle_hops, CHUNK, cut=CHUNK // 2)
     for distance, first, count, value in shares:
         chunk = first // CHUNK + 2
-        keep(value, 0, distance, chunk, spots + 1 - chunk, 0, CHUNK)
+        keep(value, 0, distance, chunk, spots + 1 - chunk, first % CHUNK, count)
+    done = [share[3] for share in shares if share[0].bit_count() > 1 and share[1] % CHUNK == 0]
     done = done + [value for one in trailing for value in one.values()]
     inner_hops = hop([inner], done)
-
-    def rows_from(first_spot, carried):
-        fits = range(first_spot - 1, first_spot + spots // 2 + 1)
-        chosen = [load for load in loads if load[3] in fits and load[4] in fits]
-        chosen.sort(key=lambda load: min(load[3:5]))
-        used = sorted({load[0] for load in chosen if load[0] is not None})
-        sources = [
-            (None if load[0] is None else used.index(load[0]),) + load[1:] for load in chosen
-        ]
+    def rows_from(call, carried):
+        first_spot, spot_count = call
+        fits = range(first_spot - 1, first_spot + spot_count + 1)
+        chosen = []
+        for load in loads:
+            if load[3] in fits and load[4] in fits:
+                chosen.append(load)
+            elif load[3] in fits:
+                key = (load[2], load[3]) + load[5:]
+                twin = [other for other in loads if (other[2], other[4]) + other[5:] == key]
+                chosen.append(
+                    ((load[0], twin[0][0]), (load[1], twin[0][1])) + (load[2], load[3], load[3]) + load[5:]
+                )
+        chosen.sort(key=lambda load: (min(load[3:5]), load[5]))
+        used = set()
+        for load in chosen:
+            used.update(load[0] if isinstance(load[0], tuple) else (load[0],))
+        used = sorted(used - {None})
+
+        def place_of(piece):
+            if isinstance(piece, tuple):
+                return tuple(used.index(one) for one in piece)
+            return None if piece is None else used.index(piece)
+
+        sources = [(place_of(load[0]),) + load[1:] for load in chosen]
         return square_rows(
             first_spot,
-            spots // 2,
+            spot_count,
             sources,
             [pieces[index] for index in used],
             tables,
             flat,
             bases,
             carried,
-            first_spot > 1,
+            call == calls[-1],
             slots,
             kslots,
             col_count,
         )
 
+    led = [value for one in leading for value in one.values()]
+    pattern = after(pattern, *led)
+    anchors = after(anchors, *led)
     look = slot_lookup(pattern, first_row, rows, total_rows, col_place, col_count, slots, core)
-    look = in_spots(jnp.transpose(look, (0, 2, 1)), core).reshape(2, -1)
+    look = in_spots(jnp.transpose(look, (0, 2, 1)), core).reshape(spots, -1)
+    calls = [(2, spots // 2 - 1), (1, 1), (spots // 2 + 1, spots // 2)]
     span = CHUNK * kslots
-    skipped = jnp.arange(2, dtype=jnp.int32)[:, None] * (spots // 2 * span)
-    look = jnp.where(look < 0, (spots // 2 + 2) * span, look - skipped).reshape(-1)
+    skipped, spare = [0] * spots, [0] * spots
+    for first_spot, count in calls:
+        for spot in range(first_spot, first_spot + count):
+            skipped[spot - 1] = (first_spot - 1) * span
+            spare[spot - 1] = (count + 2) * span
+    skipped = jnp.array(skipped, jnp.int32)[:, None]
+    spare = jnp.array(spare, jnp.int32)[:, None]
+    look = jnp.where(look < 0, spare, look - skipped).reshape(-1)
     own_anchors = lax.dynamic_slice(anchors, (0, first_row, col_place * slots), (3, rows, slots))
     own_anchors = in_spots(jnp.transpose(own_anchors, (1, 0, 2)), core)
     own_anchors = jnp.transpose(own_anchors, (1, 0, 2)).reshape(3, rows * slots)
@@ -414,16 +461,16 @@
     tables = [jnp.reshape(core, (1,)), look, planes, lines, turns]
     bases = [basis_x, basis_yz]
 
-    early = rows_from(1, None)
+    early = rows_from(calls[0], None)
     shares, _ = shares_of([inner], inner_hops, CHUNK, early[1:2])
+    halfway = rows_from(calls[1], early)
     for distance, first, count, value in shares:
         keep(value, 0, distance, spots, spots, first, count)
     for distance, first, count, value in [(0, 0, CHUNK, inner)] + shares:
-        if distance.bit_count() < 2:
-            value = after(value, early[1])
-        come = links.send("inside", value, 2, moves["inside"])
+        value = after(value, (early if distance.bit_count() < 2 else halfway)[1])
+        come = moves["inside"](value)
         keep(come, 0, distance, spots + 1, spots + 1, first, count)
-    square, middle_planes, low, high = rows_from(1 + spots // 2, early)
+    square, middle_planes, low, high = rows_from(calls[2], halfway)
 
     wire = jnp.bfloat16
     rims = [from_behind(high, "row", 1), from_behind(low, "row", -1)]
@@ -432,7 +479,7 @@
     share = LANES // col_count
     by_share = folded.reshape(col_count, share, PL, LANES)
     total = lax.dynamic_index_in_dim(by_share, col_place, 0, keepdims=False)
-    for distance in range(1, col_count):
+    for distance in sorted(range(1, col_count), key=lambda d: -d.bit_count()):
         sent = lax.dynamic_index_in_dim(by_share, col_place ^ distance, 0, keepdims=False)
         total = total + across(sent.astype(wire), "col", distance).astype(jnp.float32)
     return square, jnp.transpose(total, (1, 0, 2))

time: 208 us -> 187 us (0.90)
  waiting for transfers between devices: 122 us -> 97.7 us
  Pallas kernels: 40.9 us -> 33.6 us
  local copies, waits for them, and re-layouts: 6.99 us -> 12.4 us
  other arithmetic: 6.35 us -> 9.36 us
  starting transfers between devices: 30.4 us -> 32.9 us
    ppermute x22 -> x24, waiting for transfers between devices: 116 us -> 85.3 us  [across(): return lax.ppermute(value, axis, [(i, i ^ flip) for i in range(peers)])]
    ppermute x2, waiting for transfers between devices: 0.01 us -> 7.77 us  [between_chips(): lax.ppermute(value, axis, [(i, (i + (1 if i % 2 else -1)) % peers) for i...]
    pallas_call x2 -> x3, Pallas kernels: 40.9 us -> 33.6 us  [square_rows(): pl.pallas_call(kernel, out_shape=out_shape, in_specs=specs, out_specs=(an...]
    unnamed x40 -> x35, local copies, waits for them, and re-layouts: 0.97 us -> 5.37 us
    slice x0 -> x1, other arithmetic: none -> 3.94 us  [per_device(): flat[n * CHUNK * slots:(n + 1) * CHUNK * slots]]
    ppermute x22 -> x24, starting transfers between devices: 23.2 us -> 26.3 us  [across(): return lax.ppermute(value, axis, [(i, i ^ flip) for i in range(peers)])]
  transfers between devices with their start and end apart: 26 -> 28, of which waited for: 15 -> 16; matrix products, arithmetic and copies ran while one was open for 3% -> 6% of each run, Pallas kernels for 10% -> 10%
where the time goes in v2:
time: 187 us
  waiting for transfers between devices  97.7 us (52%)
  Pallas kernels  33.6 us (18%)
  starting transfers between devices  32.9 us (18%)
  local copies, waits for them, and re-layouts  12.4 us (7%)
  other arithmetic  9.36 us (5%)
    ppermute x24, waiting for transfers between devices, across(): return lax.ppermute(value, axis, [(i, i ^ flip) for i in range(peers)])  85.3 us
    pallas_call x3, Pallas kernels, square_rows(): pl.pallas_call(kernel, out_shape=out_shape, in_specs=specs, out_specs=(an...  33.6 us
    ppermute x24, starting transfers between devices, across(): return lax.ppermute(value, axis, [(i, i ^ flip) for i in range(peers)])  26.3 us
    ppermute x2, waiting for transfers between devices, between_chips(): lax.ppermute(value, axis, [(i, (i + (1 if i % 2 else -1)) % peers) for i...  7.77 us
    unnamed x35, local copies, waits for them, and re-layouts  5.37 us
    ppermute x2, waiting for transfers between devices, from_behind(): lax.ppermute(value, axis, [(i, (i + by) % peers) for i in range(peers)])  4.7 us
    slice x1, other arithmetic, per_device(): flat[n * CHUNK * slots:(n + 1) * CHUNK * slots]  3.94 us
  transfers between devices with their start and end apart: 28, of which 16 were waited for; matrix products, arithmetic and copies ran while one was open for 6% of the time, Pallas kernels for 10%

profile of v2, /device:TPU:0, one launch (start us, length us, event | category | flops | bytes accessed | tf_op | source)
XLA Modules:
  0.0 186.9 jit_solution(2147878146461113436)
XLA Ops:
  0.7 3.9 %fusion.28 = (bf16[8,4,128,128]{3,2,1,0:T(8,128)(2,1)}, bf16[8,4,128,128]{3,2,1,0:T(8,128)(2,1)}, bf16[8,4,128,128]{3,2,1,0:T(8,128)(2,1)}) fusion(bf16[32,4,128,128]{3,2,1,0:T(8,128)(2,1)} %param.7, pred[]{:T(512)S(6)} %eq.232), kind=kLoop, calls=%fused_computation.98 | loop fusion | flops 524288 | bytes 7340033 | tf_op jit(solution)/shard_map/slice | solution.py:352
  4.6 2.9 %collective-permute-start = (bf16[32,128,128]{2,1,0:T(8,128)(2,1)}, bf16[32,128,128]{2,1,0:T(8,128)(2,1)S(1)}, u32[]{:S(2)}, u32[]{:S(2)}) collective-permute-start(bf16[32,128,128]{2,1,0:T(8,128)(2,1)} %bitcast.2), channel_id=1, source_target_pairs={{0,1},{1,0},{2,3},{3,2},{4,5},{5,4},{6,7},{7,6},{8,9},{9,8},{10,11... | collective-permute-start | bytes 3145736 | tf_op jit(solution)/shard_map/ppermute | solution.py:22
  9.1 21.8 %collective-permute-done.refs_6_.refs_1_ = bf16[32,128,128]{2,1,0:T(8,128)(2,1)S(1)} collective-permute-done((bf16[32,128,128]{2,1,0:T(8,128)(2,1)}, bf16[32,128,128]{2,1,0:T(8,128)(2,1)S(1)}, u32[]{:S(2)}, u32[]{:S(2)}) %collective-permute-start) | collective-permute-done | bytes 1048608 | tf_op jit(solution)/shard_map/ppermute | solution.py:22
  31.0 1.8 collective-permute-start.1
  32.9 1.6 collective-permute-start.3
  34.4 1.6 collective-permute-start.19
  36.0 8.1 %collective-permute-done.1.refs_8_.refs_4_ = bf16[16,128,128]{2,1,0:T(8,128)(2,1)S(1)} collective-permute-done((bf16[16,128,128]{2,1,0:T(8,128)(2,1)S(1)}, bf16[16,128,128]{2,1,0:T(8,128)(2,1)S(1)}, u32[]{:S(2)}, u32[]{:S(2)}) %collective-permute-start.1) | collective-permute-done | bytes 524320 | tf_op jit(solution)/shard_map/ppermute | solution.py:22
  50.5 3.4 %pad_maximum_fusion = bf16[96,128,128]{2,1,0:T(8,128)(2,1)} fusion(bf16[16,128,128]{2,1,0:T(8,128)(2,1)} %copy-done.5, bf16[16,128,128]{2,1,0:T(8,128)(2,1)} %copy-done.2, bf16[32,128,128]{2,1,0:T(8,128)(2,1)S(1)} %collective-permute-done.2.refs_7_.refs_3_, bf16[32,128,128]{2,1,0:T(8,128)(2,1)S(1)} %collective-permute-done.refs_6_.refs_1_), kind=kLoop, calls=%fused_computation | loop fusion | flops 4718592 | bytes 6291456 | tf_op jit(solution)/shard_map/concatenate | solution.py:383
  54.0 7.8 %collective-permute-done.19.refs_0_ = bf16[32,128,128]{2,1,0:T(8,128)(2,1)} collective-permute-done((bf16[32,128,128]{2,1,0:T(8,128)(2,1)}, bf16[32,128,128]{2,1,0:T(8,128)(2,1)}, u32[]{:S(2)}, u32[]{:S(2)}) %collective-permute-start.19) | collective-permute-done | bytes 1048608 | tf_op jit(solution)/shard_map/ppermute | solution.py:32
  63.1 2.4 %constant_dynamic-slice_fusion.3 = bf16[32,128,128]{2,1,0:T(8,128)(2,1)} fusion(bf16[128,128,128]{2,1,0:T(8,128)(2,1)} %bitcast.80, s32[]{:T(128)S(6)} %select_n.293), kind=kLoop, calls=%fused_computation.85 | loop fusion | bytes 2097156 | tf_op jit(solution)/shard_map/dynamic_slice | solution.py:344
  65.4 7.1 %collective-permute-done.5.refs_13_.refs_9_.refs_3_ = bf16[32,128,128]{2,1,0:T(8,128)(2,1)S(1)} collective-permute-done((bf16[32,128,128]{2,1,0:T(8,128)(2,1)}, bf16[32,128,128]{2,1,0:T(8,128)(2,1)S(1)}, u32[]{:S(2)}, u32[]{:S(2)}) %collective-permute-start.5) | collective-permute-done | bytes 1048608 | tf_op jit(solution)/shard_map/ppermute | solution.py:22
  75.8 2.3 %fusion.30 = (bf16[16,128,128]{2,1,0:T(8,128)(2,1)}, bf16[16,128,128]{2,1,0:T(8,128)(2,1)}) fusion(bf16[32,128,128]{2,1,0:T(8,128)(2,1)} %collective-permute-done.4.refs_10_.refs_6_.refs_0_), kind=kLoop, calls=%fused_computation.100 | loop fusion | bytes 2097152 | tf_op jit(solution)/shard_map/slice | solution.py:54
  79.6 16.6 %collective-permute-done.7.refs_12_.refs_8_.refs_2_ = bf16[32,128,128]{2,1,0:T(8,128)(2,1)} collective-permute-done((bf16[32,128,128]{2,1,0:T(8,128)(2,1)}, bf16[32,128,128]{2,1,0:T(8,128)(2,1)}, u32[]{:S(2)}, u32[]{:S(2)}) %collective-permute-start.7) | collective-permute-done | bytes 1048608 | tf_op jit(solution)/shard_map/ppermute | solution.py:22
  99.2 8.3 %collective-permute-done.10.refs_16_.refs_12_.refs_6_ = bf16[16,128,128]{2,1,0:T(8,128)(2,1)} collective-permute-done((bf16[16,128,128]{2,1,0:T(8,128)(2,1)}, bf16[16,128,128]{2,1,0:T(8,128)(2,1)}, u32[]{:S(2)}, u32[]{:S(2)}) %collective-permute-start.10) | collective-permute-done | bytes 524320 | tf_op jit(solution)/shard_map/ppermute | solution.py:22
  110.0 8.7 %collective-permute-done.11.refs_17_.refs_13_.refs_7_ = bf16[16,128,128]{2,1,0:T(8,128)(2,1)} collective-permute-done((bf16[16,128,128]{2,1,0:T(8,128)(2,1)}, bf16[16,128,128]{2,1,0:T(8,128)(2,1)}, u32[]{:S(2)}, u32[]{:S(2)}) %collective-permute-start.11) | collective-permute-done | bytes 524320 | tf_op jit(solution)/shard_map/ppermute | solution.py:22
  118.8 2.2 %copy-done.1 = bf16[32,4,128,128]{3,2,1,0:T(8,128)(2,1)S(1)} copy-done((bf16[32,4,128,128]{3,2,1,0:T(8,128)(2,1)S(1)}, bf16[32,4,128,128]{3,2,1,0:T(8,128)(2,1)}, u32[]{:S(2)}) %copy-start.1) | copy-done | bytes 4194328
  123.0 9.1 %square_and_place.3 = (f32[32,4,128,128]{3,2,1,0:T(8,128)}, f32[128,32,128]{2,1,0:T(8,128)S(1)}) custom-call(s32[1]{0:T(128)} %bitcast.refs_0_.core, s32[2048]{0:T(1024)S(1)} %subtract_select_fusion.1.refs_1_.look, s32[128]{0:T(128)S(1)} %get-tuple-element.100.refs_2_.planes, s32[128]{0:T(128)S(1)} %squeeze.15.refs_3_.lines, ...), custom_call_target="tpu_custom_call" | custom-call | flops 6442450944 | bytes 25165824 | tf_op jit(solution)/shard_map/square_and_place/pallas_call | solution.py:303
  132.3 4.5 %collective-permute-done.13.refs_9_ = bf16[32,128,128]{2,1,0:T(8,128)(2,1)S(1)} collective-permute-done((bf16[32,128,128]{2,1,0:T(8,128)(2,1)}, bf16[32,128,128]{2,1,0:T(8,128)(2,1)S(1)}, u32[]{:S(2)}, u32[]{:S(2)}) %collective-permute-start.13) | collective-permute-done | bytes 1048608 | tf_op jit(solution)/shard_map/ppermute | solution.py:22
  140.4 9.5 %square_and_place.4 = (f32[32,4,128,128]{3,2,1,0:T(8,128)}, f32[128,32,128]{2,1,0:T(8,128)S(1)}) custom-call(s32[1]{0:T(128)} %bitcast.refs_0_.core, s32[2048]{0:T(1024)S(1)} %subtract_select_fusion.1.refs_1_.look, s32[128]{0:T(128)S(1)} %get-tuple-element.100.refs_2_.planes, s32[128]{0:T(128)S(1)} %squeeze.15.refs_3_.lines, ...), custom_call_target="tpu_custom_call", output_to_operand_aliasing={{0}: (23, {})} | custom-call | flops 6442450944 | bytes 25165824 | tf_op jit(solution)/shard_map/square_and_place/pallas_call | solution.py:303
  152.6 14.9 %square_and_place.5 = (f32[32,4,128,128]{3,2,1,0:T(8,128)}, f32[128,16,128]{2,1,0:T(8,128)S(1)}, bf16[64,16,128]{2,1,0:T(8,128)(2,1)S(1)}, bf16[64,16,128]{2,1,0:T(8,128)(2,1)S(1)}) custom-call(s32[1]{0:T(128)} %bitcast.refs_0_.core, s32[2048]{0:T(1024)S(1)} %subtract_select_fusion.1.refs_1_.look, ...), custom_call_target="tpu_custom_call", output_to_operand_aliasing={{0}: (26, {})} | custom-call | flops 12884901888 | bytes 25165824 | tf_op jit(solution)/shard_map/square_and_place/pallas_call | solution.py:303
  167.8 3.4 %collective-permute-start.24 = (bf16[64,16,128]{2,1,0:T(8,128)(2,1)S(1)}, bf16[64,16,128]{2,1,0:T(8,128)(2,1)S(1)}, u32[]{:S(2)}, u32[]{:S(2)}) collective-permute-start(bf16[64,16,128]{2,1,0:T(8,128)(2,1)S(1)} %get-tuple-element.45), channel_id=1, source_target_pairs={{0,28},{4,0},{8,4},{12,8},{16,12},{20,16},{24,20},{28,24},{1,29},{... | collective-permute-start | bytes 786440 | tf_op jit(solution)/shard_map/ppermute | solution.py:27
  171.2 4.7 %collective-permute-done.23 = bf16[64,16,128]{2,1,0:T(8,128)(2,1)S(1)} collective-permute-done((bf16[64,16,128]{2,1,0:T(8,128)(2,1)S(1)}, bf16[64,16,128]{2,1,0:T(8,128)(2,1)S(1)}, u32[]{:S(2)}, u32[]{:S(2)}) %collective-permute-start.23) | collective-permute-done | bytes 262176 | tf_op jit(solution)/shard_map/ppermute | solution.py:27
  179.9 2.5 %collective-permute-done.25 = bf16[32,16,128]{2,0,1:T(8,128)(2,1)S(1)} collective-permute-done((bf16[32,16,128]{2,0,1:T(8,128)(2,1)S(1)}, bf16[32,16,128]{2,0,1:T(8,128)(2,1)S(1)}, u32[]{:S(2)}, u32[]{:S(2)}) %collective-permute-start.25) | collective-permute-done | bytes 131104 | tf_op jit(solution)/shard_map/ppermute | solution.py:22
  182.4 2.3 %collective-permute-done.26 = bf16[32,16,128]{2,0,1:T(8,128)(2,1)S(1)} collective-permute-done((bf16[32,16,128]{2,0,1:T(8,128)(2,1)S(1)}, bf16[32,16,128]{2,0,1:T(8,128)(2,1)S(1)}, u32[]{:S(2)}, u32[]{:S(2)}) %collective-permute-start.26) | collective-permute-done | bytes 131104 | tf_op jit(solution)/shard_map/ppermute | solution.py:22
  (112 shorter events, 34.2 us)
Async XLA Ops:
  4.6 26.3 %collective-permute-start = (bf16[32,128,128]{2,1,0:T(8,128)(2,1)}, bf16[32,128,128]{2,1,0:T(8,128)(2,1)S(1)}, u32[]{:S(2)}, u32[]{:S(2)}) collective-permute-start(bf16[32,128,128]{2,1,0:T(8,128)(2,1)} %bitcast.2), channel_id=1, source_target_pairs={{0,1},{1,0},{2,3},{3,2},{4,5},{5,4},{6,7},{7,6},{8,9},{9,8},{10,11... | collective-permute-start | bytes 3145736 | tf_op jit(solution)/shard_map/ppermute | solution.py:22
  7.6 25.3 %collective-permute-start.2 = (bf16[32,128,128]{2,1,0:T(8,128)(2,1)}, bf16[32,128,128]{2,1,0:T(8,128)(2,1)S(1)}, u32[]{:S(2)}, u32[]{:S(2)}) collective-permute-start(bf16[32,128,128]{2,1,0:T(8,128)(2,1)} %bitcast.2), channel_id=1, source_target_pairs={{0,2},{1,3},{2,0},{3,1},{4,6},{5,7},{6,4},{7,5},{8,10},{9,11},{10,... | collective-permute-start | bytes 3145736 | tf_op jit(solution)/shard_map/ppermute | solution.py:22
  31.0 13.2 %collective-permute-start.1 = (bf16[16,128,128]{2,1,0:T(8,128)(2,1)S(1)}, bf16[16,128,128]{2,1,0:T(8,128)(2,1)S(1)}, u32[]{:S(2)}, u32[]{:S(2)}) collective-permute-start(bf16[16,128,128]{2,1,0:T(8,128)(2,1)S(1)} %slice.172), channel_id=1, source_target_pairs={{0,2},{1,3},{2,0},{3,1},{4,6},{5,7},{6,4},{7,5},{8,10},{9,11},{10,... | collective-permute-start | bytes 1572872 | tf_op jit(solution)/shard_map/ppermute | solution.py:22
  32.9 12.6 %collective-permute-start.3 = (bf16[16,128,128]{2,1,0:T(8,128)(2,1)S(1)}, bf16[16,128,128]{2,1,0:T(8,128)(2,1)S(1)}, u32[]{:S(2)}, u32[]{:S(2)}) collective-permute-start(bf16[16,128,128]{2,1,0:T(8,128)(2,1)S(1)} %slice.173), channel_id=1, source_target_pairs={{0,1},{1,0},{2,3},{3,2},{4,5},{5,4},{6,7},{7,6},{8,9},{9,8},{10,11... | collective-permute-start | bytes 1572872 | tf_op jit(solution)/shard_map/ppermute | solution.py:22
  34.4 27.3 %collective-permute-start.19 = (bf16[32,128,128]{2,1,0:T(8,128)(2,1)}, bf16[32,128,128]{2,1,0:T(8,128)(2,1)}, u32[]{:S(2)}, u32[]{:S(2)}) collective-permute-start(bf16[32,128,128]{2,1,0:T(8,128)(2,1)} %bitcast.2), channel_id=1, source_target_pairs={{0,28},{4,8},{8,4},{12,16},{16,12},{20,24},{24,20},{28,0},{1,29},{... | collective-permute-start | bytes 3145736 | tf_op jit(solution)/shard_map/ppermute | solution.py:32
  46.3 26.3 %collective-permute-start.5 = (bf16[32,128,128]{2,1,0:T(8,128)(2,1)}, bf16[32,128,128]{2,1,0:T(8,128)(2,1)S(1)}, u32[]{:S(2)}, u32[]{:S(2)}) collective-permute-start(bf16[32,128,128]{2,1,0:T(8,128)(2,1)} %bitcast.3), channel_id=1, source_target_pairs={{0,2},{1,3},{2,0},{3,1},{4,6},{5,7},{6,4},{7,5},{8,10},{9,11},{10,... | collective-permute-start | bytes 3145736 | tf_op jit(solution)/shard_map/ppermute | solution.py:22
  47.4 27.7 %collective-permute-start.4 = (bf16[32,128,128]{2,1,0:T(8,128)(2,1)}, bf16[32,128,128]{2,1,0:T(8,128)(2,1)}, u32[]{:S(2)}, u32[]{:S(2)}) collective-permute-start(bf16[32,128,128]{2,1,0:T(8,128)(2,1)} %bitcast.1), channel_id=1, source_target_pairs={{0,1},{1,0},{2,3},{3,2},{4,5},{5,4},{6,7},{7,6},{8,9},{9,8},{10,11... | collective-permute-start | bytes 3145736 | tf_op jit(solution)/shard_map/ppermute | solution.py:22
  48.5 47.8 %collective-permute-start.7 = (bf16[32,128,128]{2,1,0:T(8,128)(2,1)}, bf16[32,128,128]{2,1,0:T(8,128)(2,1)}, u32[]{:S(2)}, u32[]{:S(2)}) collective-permute-start(bf16[32,128,128]{2,1,0:T(8,128)(2,1)} %bitcast.3), channel_id=1, source_target_pairs={{0,1},{1,0},{2,3},{3,2},{4,5},{5,4},{6,7},{7,6},{8,9},{9,8},{10,11... | collective-permute-start | bytes 3145736 | tf_op jit(solution)/shard_map/ppermute | solution.py:22
  49.6 47.6 %collective-permute-start.6 = (bf16[32,128,128]{2,1,0:T(8,128)(2,1)}, bf16[32,128,128]{2,1,0:T(8,128)(2,1)}, u32[]{:S(2)}, u32[]{:S(2)}) collective-permute-start(bf16[32,128,128]{2,1,0:T(8,128)(2,1)} %bitcast.1), channel_id=1, source_target_pairs={{0,2},{1,3},{2,0},{3,1},{4,6},{5,7},{6,4},{7,5},{8,10},{9,11},{10,... | collective-permute-start | bytes 3145736 | tf_op jit(solution)/shard_map/ppermute | solution.py:22
  61.7 78.1 %collective-permute-start.20 = (bf16[96,128,128]{2,1,0:T(8,128)(2,1)}, bf16[96,128,128]{2,1,0:T(8,128)(2,1)}, u32[]{:S(2)}, u32[]{:S(2)}) collective-permute-start(bf16[96,128,128]{2,1,0:T(8,128)(2,1)} %pad_maximum_fusion), channel_id=1, source_target_pairs={{0,28},{4,8},{8,4},{12,16},{16,12},{20,24},{24,20},{28,0},{1,29},{... | collective-permute-start | bytes 9437192 | tf_op jit(solution)/shard_map/ppermute | solution.py:32
  73.6 33.9 %collective-permute-start.10 = (bf16[16,128,128]{2,1,0:T(8,128)(2,1)}, bf16[16,128,128]{2,1,0:T(8,128)(2,1)}, u32[]{:S(2)}, u32[]{:S(2)}) collective-permute-start(bf16[16,128,128]{2,1,0:T(8,128)(2,1)} %get-tuple-element.55), channel_id=1, source_target_pairs={{0,1},{1,0},{2,3},{3,2},{4,5},{5,4},{6,7},{7,6},{8,9},{9,8},{10,11... | collective-permute-start | bytes 1572872 | tf_op jit(solution)/shard_map/ppermute | solution.py:22
  78.1 29.5 %collective-permute-start.8 = (bf16[16,128,128]{2,1,0:T(8,128)(2,1)}, bf16[16,128,128]{2,1,0:T(8,128)(2,1)}, u32[]{:S(2)}, u32[]{:S(2)}) collective-permute-start(bf16[16,128,128]{2,1,0:T(8,128)(2,1)} %get-tuple-element.57), channel_id=1, source_target_pairs={{0,2},{1,3},{2,0},{3,1},{4,6},{5,7},{6,4},{7,5},{8,10},{9,11},{10,... | collective-permute-start | bytes 1572872 | tf_op jit(solution)/shard_map/ppermute | solution.py:22
  96.3 22.5 %collective-permute-start.11 = (bf16[16,128,128]{2,1,0:T(8,128)(2,1)}, bf16[16,128,128]{2,1,0:T(8,128)(2,1)}, u32[]{:S(2)}, u32[]{:S(2)}) collective-permute-start(bf16[16,128,128]{2,1,0:T(8,128)(2,1)} %get-tuple-element.54), channel_id=1, source_target_pairs={{0,1},{1,0},{2,3},{3,2},{4,5},{5,4},{6,7},{7,6},{8,9},{9,8},{10,11... | collective-permute-start | bytes 1572872 | tf_op jit(solution)/shard_map/ppermute | solution.py:22
  97.2 21.5 %collective-permute-start.9 = (bf16[16,128,128]{2,1,0:T(8,128)(2,1)}, bf16[16,128,128]{2,1,0:T(8,128)(2,1)}, u32[]{:S(2)}, u32[]{:S(2)}) collective-permute-start(bf16[16,128,128]{2,1,0:T(8,128)(2,1)} %get-tuple-element.56), channel_id=1, source_target_pairs={{0,2},{1,3},{2,0},{3,1},{4,6},{5,7},{6,4},{7,5},{8,10},{9,11},{10,... | collective-permute-start | bytes 1572872 | tf_op jit(solution)/shard_map/ppermute | solution.py:22
  107.5 29.3 %collective-permute-start.13 = (bf16[32,128,128]{2,1,0:T(8,128)(2,1)}, bf16[32,128,128]{2,1,0:T(8,128)(2,1)S(1)}, u32[]{:S(2)}, u32[]{:S(2)}) collective-permute-start(bf16[32,128,128]{2,1,0:T(8,128)(2,1)} %constant_dynamic-slice_fusion.3), channel_id=1, source_target_pairs={{0,2},{1,3},{2,0},{3,1},{4,6},{5,7},{6,4},{7,5},{8,10},{9,11},{10,... | collective-permute-start | bytes 3145736 | tf_op jit(solution)/shard_map/ppermute | solution.py:22
  108.5 30.2 %collective-permute-start.12 = (bf16[32,128,128]{2,1,0:T(8,128)(2,1)}, bf16[32,128,128]{2,1,0:T(8,128)(2,1)S(1)}, u32[]{:S(2)}, u32[]{:S(2)}) collective-permute-start(bf16[32,128,128]{2,1,0:T(8,128)(2,1)} %constant_dynamic-slice_fusion.3), channel_id=1, source_target_pairs={{0,1},{1,0},{2,3},{3,2},{4,5},{5,4},{6,7},{7,6},{8,9},{9,8},{10,11... | collective-permute-start | bytes 3145736 | tf_op jit(solution)/shard_map/ppermute | solution.py:22
  132.2 18.3 %collective-permute-start.16 = (bf16[32,128,128]{2,1,0:T(8,128)(2,1)S(1)}, bf16[32,128,128]{2,1,0:T(8,128)(2,1)S(1)}, u32[]{:S(2)}, u32[]{:S(2)}) collective-permute-start(bf16[32,128,128]{2,1,0:T(8,128)(2,1)S(1)} %copy-done.10), channel_id=1, source_target_pairs={{0,4},{4,0},{8,12},{12,8},{16,20},{20,16},{24,28},{28,24},{1,5},{5... | collective-permute-start | bytes 3145736 | tf_op jit(solution)/shard_map/ppermute | solution.py:22
  136.8 13.0 %collective-permute-start.15 = (bf16[16,128,128]{2,1,0:T(8,128)(2,1)S(1)}, bf16[16,128,128]{2,1,0:T(8,128)(2,1)S(1)}, u32[]{:S(2)}, u32[]{:S(2)}) collective-permute-start(bf16[16,128,128]{2,1,0:T(8,128)(2,1)S(1)} %slice.202), channel_id=1, source_target_pairs={{0,1},{1,0},{2,3},{3,2},{4,5},{5,4},{6,7},{7,6},{8,9},{9,8},{10,11... | collective-permute-start | bytes 1572872 | tf_op jit(solution)/shard_map/ppermute | solution.py:22
  138.8 11.2 %collective-permute-start.14 = (bf16[16,128,128]{2,1,0:T(8,128)(2,1)S(1)}, bf16[16,128,128]{2,1,0:T(8,128)(2,1)S(1)}, u32[]{:S(2)}, u32[]{:S(2)}) collective-permute-start(bf16[16,128,128]{2,1,0:T(8,128)(2,1)S(1)} %slice.201), channel_id=1, source_target_pairs={{0,2},{1,3},{2,0},{3,1},{4,6},{5,7},{6,4},{7,5},{8,10},{9,11},{10,... | collective-permute-start | bytes 1572872 | tf_op jit(solution)/shard_map/ppermute | solution.py:22
  139.9 12.8 %collective-permute-start.18 = (bf16[32,128,128]{2,1,0:T(8,128)(2,1)S(1)}, bf16[32,128,128]{2,1,0:T(8,128)(2,1)S(1)}, u32[]{:S(2)}, u32[]{:S(2)}) collective-permute-start(bf16[32,128,128]{2,1,0:T(8,128)(2,1)S(1)} %collective-permute-done.13.refs_9_), channel_id=1, source_target_pairs={{0,4},{4,0},{8,12},{12,8},{16,20},{20,16},{24,28},{28,24},{1,5},{5... | collective-permute-start | bytes 3145736 | tf_op jit(solution)/shard_map/ppermute | solution.py:22
  139.9 12.8 %collective-permute-start.17 = (bf16[32,128,128]{2,1,0:T(8,128)(2,1)S(1)}, bf16[32,128,128]{2,1,0:T(8,128)(2,1)S(1)}, u32[]{:S(2)}, u32[]{:S(2)}) collective-permute-start(bf16[32,128,128]{2,1,0:T(8,128)(2,1)S(1)} %collective-permute-done.12.refs_8_), channel_id=1, source_target_pairs={{0,4},{4,0},{8,12},{12,8},{16,20},{20,16},{24,28},{28,24},{1,5},{5... | collective-permute-start | bytes 3145736 | tf_op jit(solution)/shard_map/ppermute | solution.py:22
  167.6 8.3 %collective-permute-start.23 = (bf16[64,16,128]{2,1,0:T(8,128)(2,1)S(1)}, bf16[64,16,128]{2,1,0:T(8,128)(2,1)S(1)}, u32[]{:S(2)}, u32[]{:S(2)}) collective-permute-start(bf16[64,16,128]{2,1,0:T(8,128)(2,1)S(1)} %get-tuple-element.44), channel_id=1, source_target_pairs={{0,4},{4,8},{8,12},{12,16},{16,20},{20,24},{24,28},{28,0},{1,5},{5... | collective-permute-start | bytes 786440 | tf_op jit(solution)/shard_map/ppermute | solution.py:27
  167.8 8.1 %collective-permute-start.24 = (bf16[64,16,128]{2,1,0:T(8,128)(2,1)S(1)}, bf16[64,16,128]{2,1,0:T(8,128)(2,1)S(1)}, u32[]{:S(2)}, u32[]{:S(2)}) collective-permute-start(bf16[64,16,128]{2,1,0:T(8,128)(2,1)S(1)} %get-tuple-element.45), channel_id=1, source_target_pairs={{0,28},{4,0},{8,4},{12,8},{16,12},{20,16},{24,20},{28,24},{1,29},{... | collective-permute-start | bytes 786440 | tf_op jit(solution)/shard_map/ppermute | solution.py:27
  178.7 7.3 %collective-permute-start.27 = (bf16[32,16,128]{2,0,1:T(8,128)(2,1)S(1)}, bf16[32,16,128]{2,0,1:T(8,128)(2,1)S(1)}, u32[]{:S(2)}, u32[]{:S(2)}) collective-permute-start(bf16[32,16,128]{2,0,1:T(8,128)(2,1)S(1)} %bitcast.98), channel_id=1, source_target_pairs={{0,2},{1,3},{2,0},{3,1},{4,6},{5,7},{6,4},{7,5},{8,10},{9,11},{10,... | collective-permute-start | bytes 393224 | tf_op jit(solution)/shard_map/ppermute | solution.py:22
  (18 other events, 365.2 us)
